TPU v7x, 32 devices: a whole 2x2x4 slice. The times are simulated.
32 devices in a mesh: row: 4 (over x, core), col: 8 (over z, y).
Axes of the slice: x: 2, y: 2, z: 4, core: 2. Of those that a mesh axis runs over, the one named last changes fastest.
Arguments:
- queries: float32 [32, 16384], P(None, ('row', 'col'))
- block_spots: int32 [4, 8, 256], P('row', 'col'), may hold values from 0 to 511, as said below
- live_blocks: int32 [4, 8], P('row', 'col'), may hold values from 1 to 256, as said below
- neighbor_cols: int32 [4, 8, 256, 16, 128], P('row', 'col'), may hold values from 0 to 127
- neighbor_sims: bfloat16 [4, 8, 256, 16, 128], P('row', 'col'), may hold values from 0.099609375 to 1
Outputs:
- solution: float32 [32, 16384], P(None, ('row', 'col'))
- residual: float32 [32, 16384], P(None, ('row', 'col'))
Inputs may be any that keep to these rules, and one draw needn't show every extreme that they name: `block_spots`: within each index of the first two dimensions the 256 spots are distinct. `live_blocks`: some index of the array holds exactly 256.
All inputs are finite; a program needn't handle non-finite values.
Results may differ from a plain program's by a relative error of at most 0.01.
Values may be sent and summed in bfloat16 or wider, within the bound.
No kernel may reach another device: no remote copies, remote signals or barrier semaphores. Data moves between devices by JAX's collectives and lax.ppermute only.
A program may use at most 128 MiB of HBM per device.

v0:
```python
import jax
import jax.numpy as jnp
from jax import lax
from jax.sharding import PartitionSpec as P

ITERS = 2


graph_weight = 0.95


def fill_blocks(neighbor_idx, neighbor_val):
    lane_ids = jnp.arange(128, dtype=jnp.int32)
    running = jnp.zeros((neighbor_idx.shape[0], 128, 128), jnp.float32)
    for column_slot in range(neighbor_idx.shape[1]):
        matched = neighbor_idx[:, column_slot, :, None] == lane_ids
        running = running + jnp.where(
            matched, neighbor_val[:, column_slot, :, None].astype(jnp.float32), jnp.float32(0.0)
        )
    return running.astype(jnp.bfloat16)


def fill_group(group_pair):
    return fill_blocks(group_pair[0], group_pair[1])


def build_blocks(index_table, value_table):
    slot_count = index_table.shape[0]
    index_groups = index_table.reshape(slot_count // 16, 16, index_table.shape[1], 128)
    value_groups = value_table.reshape(slot_count // 16, 16, value_table.shape[1], 128)
    return lax.map(fill_group, (index_groups, value_groups)).reshape(slot_count, 128, 128)


def spd_solve(matrix, right_side):
    factor = jnp.linalg.cholesky(matrix)
    partial_value = lax.linalg.triangular_solve(factor, right_side, left_side=True, lower=True)
    return lax.linalg.triangular_solve(
        factor, partial_value, left_side=True, lower=True, transpose_a=True
    )


def gram_matrix(first_rows, second_rows):
    return lax.dot_general(
        first_rows, second_rows, (((1,), (1,)), ((), ())), precision=lax.Precision.HIGHEST
    )


def symmetric(square):
    return 0.5 * (square + square.T)


def block_products(blocks, spot_list, slot_start, slot_stop, col_dirs, row_dirs):
    query_rows = col_dirs.shape[0]
    row_blocks = row_dirs.shape[1]
    col_blocks = col_dirs.shape[1]
    row_lanes = jnp.arange(row_blocks, dtype=jnp.int32)
    col_lanes = jnp.arange(col_blocks, dtype=jnp.int32)

    def group_turn(turn_index, totals):
        row_total, col_total = totals
        first_slot = turn_index * 16
        group_blocks = lax.dynamic_slice_in_dim(blocks, first_slot, 16, 0)
        group_spots = lax.dynamic_slice_in_dim(spot_list, first_slot, 16, 0)
        slot_ids = first_slot + jnp.arange(16, dtype=jnp.int32)
        active = ((slot_ids >= slot_start) & (slot_ids < slot_stop)).astype(jnp.float32)
        block_row = group_spots // col_blocks
        block_col = group_spots % col_blocks
        col_vecs = jnp.take(col_dirs, block_col, axis=1)
        row_vecs = jnp.take(row_dirs, block_row, axis=1)
        forward = jnp.einsum(
            "sij,msj->msi", group_blocks, col_vecs, preferred_element_type=jnp.float32
        )
        backward = jnp.einsum(
            "sij,msi->msj", group_blocks, row_vecs, preferred_element_type=jnp.float32
        )
        row_select = (block_row[:, None] == row_lanes).astype(jnp.float32) * active[:, None]
        col_select = (block_col[:, None] == col_lanes).astype(jnp.float32) * active[:, None]
        row_total = row_total + jnp.einsum(
            "sb,msi->mbi", row_select, forward, precision=lax.Precision.HIGHEST
        )
        col_total = col_total + jnp.einsum(
            "sb,msi->mbi", col_select, backward, precision=lax.Precision.HIGHEST
        )
        return (row_total, col_total)

    row_zero = jnp.zeros((query_rows, row_blocks, 128), jnp.float32)
    col_zero = jnp.zeros((query_rows, col_blocks, 128), jnp.float32)
    return lax.fori_loop(slot_start // 16, (slot_stop + 15) // 16, group_turn, (row_zero, col_zero))


def body(queries, block_spots, live_blocks, neighbor_cols, neighbor_sims):
    row_count = lax.axis_size("row")
    col_count = lax.axis_size("col")
    seg_len = queries.shape[1]
    per_seg = seg_len // 128
    row_blocks = row_count * per_seg
    col_blocks = col_count * per_seg
    spot_list = block_spots[0, 0]
    live_count = live_blocks[0, 0]
    index_table = neighbor_cols[0, 0]
    value_table = neighbor_sims[0, 0]
    blocks = build_blocks(index_table, value_table)

    def partial_sums(col_dirs, row_dirs):
        query_rows = col_dirs.shape[0]
        row_total, col_total = block_products(
            blocks, spot_list, jnp.int32(0), live_count, col_dirs, row_dirs
        )
        row_sum = lax.psum_scatter(
            row_total.reshape(query_rows, row_blocks * 128), "row", scatter_dimension=1, tiled=True
        )
        col_sum = lax.psum_scatter(
            col_total.reshape(query_rows, col_blocks * 128), "col", scatter_dimension=1, tiled=True
        )
        return 0.5 * (row_sum + col_sum)

    unit_cols = jnp.ones((1, col_blocks, 128), jnp.bfloat16)
    unit_rows = jnp.ones((1, row_blocks, 128), jnp.bfloat16)
    degree = 1.0 + partial_sums(unit_cols, unit_rows)
    scaling = 1.0 / jnp.sqrt(degree)
    solution = jnp.zeros_like(queries)
    residual = queries
    direction = queries

    def residual_gram(current):
        return symmetric(lax.psum(gram_matrix(current, current), ("row", "col")))

    res_gram = residual_gram(residual)
    for sweep_index in range(ITERS):
        scaled = (scaling * direction).astype(jnp.bfloat16)
        operator_query_rows = scaled.shape[0]
        operator_col_dirs = lax.all_gather(scaled, "col", axis=1, tiled=True).reshape(
            operator_query_rows, col_blocks, 128
        )
        operator_row_dirs = lax.all_gather(scaled, "row", axis=1, tiled=True).reshape(
            operator_query_rows, row_blocks, 128
        )
        applied = direction - graph_weight * scaling * partial_sums(
            operator_col_dirs, operator_row_dirs
        )
        curvature = symmetric(lax.psum(gram_matrix(direction, applied), ("row", "col")))
        weights = spd_solve(curvature, res_gram)
        solution = solution + jnp.dot(weights.T, direction, precision=lax.Precision.HIGHEST)
        residual = residual - jnp.dot(weights.T, applied, precision=lax.Precision.HIGHEST)
        if sweep_index + 1 < ITERS:
            new_gram = residual_gram(residual)
            mixing = spd_solve(res_gram, new_gram)
            direction = residual + jnp.dot(mixing.T, direction, precision=lax.Precision.HIGHEST)
            res_gram = new_gram
    return (solution, residual)


def solution(mesh):
    placed = (
        P(None, ("row", "col")),
        P("row", "col", None),
        P("row", "col"),
        P("row", "col", None, None, None),
        P("row", "col", None, None, None),
    )
    return jax.shard_map(
        body,
        mesh=mesh,
        in_specs=placed,
        out_specs=(P(None, ("row", "col")), P(None, ("row", "col"))),
        check_vma=False,
    )
```

profile of v0, /device:TPU:0, one launch (start us, length us, event | category | flops | bytes accessed | tf_op | source)
XLA Modules:
  0.0 972.4 jit_solution(15600554730261440772)
XLA Ops:
  7.9 190.7 %while.55 = (s32[]{:T(128)}, bf16[16,16,128,128]{3,2,1,0:T(8,128)(2,1)}, s32[16,16,16,128]{3,2,1,0:T(8,128)}, bf16[16,16,16,128]{3,2,1,0:T(8,128)(2,1)}, s32[]{:T(128)}) while((s32[]{:T(128)}, bf16[16,16,128,128]{3,2,1,0:T(8,128)(2,1)}, s32[16,16,16,128]{3,2,1,0:T(8,128)}, bf16[16,16,16,128]{3,2,1,0:T(8,128)(2,1)}, s32[]{:T(128)}) %tuple.194), condition=%wide.region_1.2_spmd, body=%wide.region_0.1_spmd.sunk | while | flops 12615682 | bytes 2032197 | solution.py:31
  9.8 10.0 %fusion.202 = bf16[16,16,128,128]{3,2,1,0:T(8,128)(2,1)} fusion(bf16[16,16,128,128]{3,2,1,0:T(8,128)(2,1)} %get-tuple-element.953, s32[]{:T(128)} %get-tuple-element.952, f32[16,128]{1,0:T(8,128)S(1)} %get-tuple-element.872, s32[16,128]{1,0:T(8,128)S(1)} %get-tuple-element.873, f32[16,128]{1,0:T(8,128)S(1)} %get-tuple-element.874, ...), kind=kLoop, calls=%fused_computation.29.clone.1 | loop fusion | flops 12582912 | bytes 786944 | tf_op jit(solution)/shard_map/while/body/jit(dynamic_update_index_in_dim)/dynamic_update_slice | solution.py:31
  21.7 10.0 %fusion.202 = bf16[16,16,128,128]{3,2,1,0:T(8,128)(2,1)} fusion(bf16[16,16,128,128]{3,2,1,0:T(8,128)(2,1)} %get-tuple-element.953, s32[]{:T(128)} %get-tuple-element.952, f32[16,128]{1,0:T(8,128)S(1)} %get-tuple-element.872, s32[16,128]{1,0:T(8,128)S(1)} %get-tuple-element.873, f32[16,128]{1,0:T(8,128)S(1)} %get-tuple-element.874, ...), kind=kLoop, calls=%fused_computation.29.clone.1 | loop fusion | flops 12582912 | bytes 786944 | tf_op jit(solution)/shard_map/while/body/jit(dynamic_update_index_in_dim)/dynamic_update_slice | solution.py:31
  33.6 10.0 %fusion.202 = bf16[16,16,128,128]{3,2,1,0:T(8,128)(2,1)} fusion(bf16[16,16,128,128]{3,2,1,0:T(8,128)(2,1)} %get-tuple-element.953, s32[]{:T(128)} %get-tuple-element.952, f32[16,128]{1,0:T(8,128)S(1)} %get-tuple-element.872, s32[16,128]{1,0:T(8,128)S(1)} %get-tuple-element.873, f32[16,128]{1,0:T(8,128)S(1)} %get-tuple-element.874, ...), kind=kLoop, calls=%fused_computation.29.clone.1 | loop fusion | flops 12582912 | bytes 786944 | tf_op jit(solution)/shard_map/while/body/jit(dynamic_update_index_in_dim)/dynamic_update_slice | solution.py:31
  45.6 10.0 %fusion.202 = bf16[16,16,128,128]{3,2,1,0:T(8,128)(2,1)} fusion(bf16[16,16,128,128]{3,2,1,0:T(8,128)(2,1)} %get-tuple-element.953, s32[]{:T(128)} %get-tuple-element.952, f32[16,128]{1,0:T(8,128)S(1)} %get-tuple-element.872, s32[16,128]{1,0:T(8,128)S(1)} %get-tuple-element.873, f32[16,128]{1,0:T(8,128)S(1)} %get-tuple-element.874, ...), kind=kLoop, calls=%fused_computation.29.clone.1 | loop fusion | flops 12582912 | bytes 786944 | tf_op jit(solution)/shard_map/while/body/jit(dynamic_update_index_in_dim)/dynamic_update_slice | solution.py:31
  57.5 10.0 %fusion.202 = bf16[16,16,128,128]{3,2,1,0:T(8,128)(2,1)} fusion(bf16[16,16,128,128]{3,2,1,0:T(8,128)(2,1)} %get-tuple-element.953, s32[]{:T(128)} %get-tuple-element.952, f32[16,128]{1,0:T(8,128)S(1)} %get-tuple-element.872, s32[16,128]{1,0:T(8,128)S(1)} %get-tuple-element.873, f32[16,128]{1,0:T(8,128)S(1)} %get-tuple-element.874, ...), kind=kLoop, calls=%fused_computation.29.clone.1 | loop fusion | flops 12582912 | bytes 786944 | tf_op jit(solution)/shard_map/while/body/jit(dynamic_update_index_in_dim)/dynamic_update_slice | solution.py:31
  69.4 10.0 %fusion.202 = bf16[16,16,128,128]{3,2,1,0:T(8,128)(2,1)} fusion(bf16[16,16,128,128]{3,2,1,0:T(8,128)(2,1)} %get-tuple-element.953, s32[]{:T(128)} %get-tuple-element.952, f32[16,128]{1,0:T(8,128)S(1)} %get-tuple-element.872, s32[16,128]{1,0:T(8,128)S(1)} %get-tuple-element.873, f32[16,128]{1,0:T(8,128)S(1)} %get-tuple-element.874, ...), kind=kLoop, calls=%fused_computation.29.clone.1 | loop fusion | flops 12582912 | bytes 786944 | tf_op jit(solution)/shard_map/while/body/jit(dynamic_update_index_in_dim)/dynamic_update_slice | solution.py:31
  81.3 10.0 %fusion.202 = bf16[16,16,128,128]{3,2,1,0:T(8,128)(2,1)} fusion(bf16[16,16,128,128]{3,2,1,0:T(8,128)(2,1)} %get-tuple-element.953, s32[]{:T(128)} %get-tuple-element.952, f32[16,128]{1,0:T(8,128)S(1)} %get-tuple-element.872, s32[16,128]{1,0:T(8,128)S(1)} %get-tuple-element.873, f32[16,128]{1,0:T(8,128)S(1)} %get-tuple-element.874, ...), kind=kLoop, calls=%fused_computation.29.clone.1 | loop fusion | flops 12582912 | bytes 786944 | tf_op jit(solution)/shard_map/while/body/jit(dynamic_update_index_in_dim)/dynamic_update_slice | solution.py:31
  93.2 10.0 %fusion.202 = bf16[16,16,128,128]{3,2,1,0:T(8,128)(2,1)} fusion(bf16[16,16,128,128]{3,2,1,0:T(8,128)(2,1)} %get-tuple-element.953, s32[]{:T(128)} %get-tuple-element.952, f32[16,128]{1,0:T(8,128)S(1)} %get-tuple-element.872, s32[16,128]{1,0:T(8,128)S(1)} %get-tuple-element.873, f32[16,128]{1,0:T(8,128)S(1)} %get-tuple-element.874, ...), kind=kLoop, calls=%fused_computation.29.clone.1 | loop fusion | flops 12582912 | bytes 786944 | tf_op jit(solution)/shard_map/while/body/jit(dynamic_update_index_in_dim)/dynamic_update_slice | solution.py:31
  105.1 10.0 %fusion.202 = bf16[16,16,128,128]{3,2,1,0:T(8,128)(2,1)} fusion(bf16[16,16,128,128]{3,2,1,0:T(8,128)(2,1)} %get-tuple-element.953, s32[]{:T(128)} %get-tuple-element.952, f32[16,128]{1,0:T(8,128)S(1)} %get-tuple-element.872, s32[16,128]{1,0:T(8,128)S(1)} %get-tuple-element.873, f32[16,128]{1,0:T(8,128)S(1)} %get-tuple-element.874, ...), kind=kLoop, calls=%fused_computation.29.clone.1 | loop fusion | flops 12582912 | bytes 786944 | tf_op jit(solution)/shard_map/while/body/jit(dynamic_update_index_in_dim)/dynamic_update_slice | solution.py:31
  117.1 10.0 %fusion.202 = bf16[16,16,128,128]{3,2,1,0:T(8,128)(2,1)} fusion(bf16[16,16,128,128]{3,2,1,0:T(8,128)(2,1)} %get-tuple-element.953, s32[]{:T(128)} %get-tuple-element.952, f32[16,128]{1,0:T(8,128)S(1)} %get-tuple-element.872, s32[16,128]{1,0:T(8,128)S(1)} %get-tuple-element.873, f32[16,128]{1,0:T(8,128)S(1)} %get-tuple-element.874, ...), kind=kLoop, calls=%fused_computation.29.clone.1 | loop fusion | flops 12582912 | bytes 786944 | tf_op jit(solution)/shard_map/while/body/jit(dynamic_update_index_in_dim)/dynamic_update_slice | solution.py:31
  129.0 10.0 %fusion.202 = bf16[16,16,128,128]{3,2,1,0:T(8,128)(2,1)} fusion(bf16[16,16,128,128]{3,2,1,0:T(8,128)(2,1)} %get-tuple-element.953, s32[]{:T(128)} %get-tuple-element.952, f32[16,128]{1,0:T(8,128)S(1)} %get-tuple-element.872, s32[16,128]{1,0:T(8,128)S(1)} %get-tuple-element.873, f32[16,128]{1,0:T(8,128)S(1)} %get-tuple-element.874, ...), kind=kLoop, calls=%fused_computation.29.clone.1 | loop fusion | flops 12582912 | bytes 786944 | tf_op jit(solution)/shard_map/while/body/jit(dynamic_update_index_in_dim)/dynamic_update_slice | solution.py:31
  140.9 10.0 %fusion.202 = bf16[16,16,128,128]{3,2,1,0:T(8,128)(2,1)} fusion(bf16[16,16,128,128]{3,2,1,0:T(8,128)(2,1)} %get-tuple-element.953, s32[]{:T(128)} %get-tuple-element.952, f32[16,128]{1,0:T(8,128)S(1)} %get-tuple-element.872, s32[16,128]{1,0:T(8,128)S(1)} %get-tuple-element.873, f32[16,128]{1,0:T(8,128)S(1)} %get-tuple-element.874, ...), kind=kLoop, calls=%fused_computation.29.clone.1 | loop fusion | flops 12582912 | bytes 786944 | tf_op jit(solution)/shard_map/while/body/jit(dynamic_update_index_in_dim)/dynamic_update_slice | solution.py:31
  152.8 10.0 %fusion.202 = bf16[16,16,128,128]{3,2,1,0:T(8,128)(2,1)} fusion(bf16[16,16,128,128]{3,2,1,0:T(8,128)(2,1)} %get-tuple-element.953, s32[]{:T(128)} %get-tuple-element.952, f32[16,128]{1,0:T(8,128)S(1)} %get-tuple-element.872, s32[16,128]{1,0:T(8,128)S(1)} %get-tuple-element.873, f32[16,128]{1,0:T(8,128)S(1)} %get-tuple-element.874, ...), kind=kLoop, calls=%fused_computation.29.clone.1 | loop fusion | flops 12582912 | bytes 786944 | tf_op jit(solution)/shard_map/while/body/jit(dynamic_update_index_in_dim)/dynamic_update_slice | solution.py:31
  164.7 10.0 %fusion.202 = bf16[16,16,128,128]{3,2,1,0:T(8,128)(2,1)} fusion(bf16[16,16,128,128]{3,2,1,0:T(8,128)(2,1)} %get-tuple-element.953, s32[]{:T(128)} %get-tuple-element.952, f32[16,128]{1,0:T(8,128)S(1)} %get-tuple-element.872, s32[16,128]{1,0:T(8,128)S(1)} %get-tuple-element.873, f32[16,128]{1,0:T(8,128)S(1)} %get-tuple-element.874, ...), kind=kLoop, calls=%fused_computation.29.clone.1 | loop fusion | flops 12582912 | bytes 786944 | tf_op jit(solution)/shard_map/while/body/jit(dynamic_update_index_in_dim)/dynamic_update_slice | solution.py:31
  176.6 10.0 %fusion.202 = bf16[16,16,128,128]{3,2,1,0:T(8,128)(2,1)} fusion(bf16[16,16,128,128]{3,2,1,0:T(8,128)(2,1)} %get-tuple-element.953, s32[]{:T(128)} %get-tuple-element.952, f32[16,128]{1,0:T(8,128)S(1)} %get-tuple-element.872, s32[16,128]{1,0:T(8,128)S(1)} %get-tuple-element.873, f32[16,128]{1,0:T(8,128)S(1)} %get-tuple-element.874, ...), kind=kLoop, calls=%fused_computation.29.clone.1 | loop fusion | flops 12582912 | bytes 786944 | tf_op jit(solution)/shard_map/while/body/jit(dynamic_update_index_in_dim)/dynamic_update_slice | solution.py:31
  188.5 10.0 %fusion.202 = bf16[16,16,128,128]{3,2,1,0:T(8,128)(2,1)} fusion(bf16[16,16,128,128]{3,2,1,0:T(8,128)(2,1)} %get-tuple-element.953, s32[]{:T(128)} %get-tuple-element.952, f32[16,128]{1,0:T(8,128)S(1)} %get-tuple-element.872, s32[16,128]{1,0:T(8,128)S(1)} %get-tuple-element.873, f32[16,128]{1,0:T(8,128)S(1)} %get-tuple-element.874, ...), kind=kLoop, calls=%fused_computation.29.clone.1 | loop fusion | flops 12582912 | bytes 786944 | tf_op jit(solution)/shard_map/while/body/jit(dynamic_update_index_in_dim)/dynamic_update_slice | solution.py:31
  198.6 37.8 %while.56 = (s32[]{:T(128)}, f32[1,16,128]{2,1,0:T(8,128)S(1)}, f32[1,32,128]{2,1,0:T(8,128)S(1)}, s32[]{:T(128)}, s32[256]{0:T(256)S(1)}, /*index=5*/bf16[256,1...) while((s32[]{:T(128)}, f32[1,16,128]{2,1,0:T(8,128)S(1)}, ...), condition=%wide.region_3.4_spmd.clone, body=%wide.region_2.3_spmd.clone.sunk | while | flops 2242742 | bytes 1193339 | solution.py:88
  240.0 71.3 %reduce-scatter.19.cloned.1.call-done = f32[512,1]{1,0:T(8,128)} async-done(((f32[2048,1]{1,0:T(8,128)}), f32[512,1]{1,0:T(8,128)}) %reduce-scatter.19.cloned.1.call-update) | async-done | bytes 2064
  312.4 71.0 %reduce-scatter.21.cloned.1.call-done = f32[512,1]{1,0:T(8,128)} async-done(((f32[4096,1]{1,0:T(8,128)}), f32[512,1]{1,0:T(8,128)}) %reduce-scatter.21.cloned.1.call-update) | async-done | bytes 2064
  384.4 30.9 %all_gather.12 = bf16[32,4096]{1,0:T(8,128)(2,1)S(1)} all-gather(bf16[32,512]{1,0:T(8,128)(2,1)S(1)} %multiply_convert_fusion.1), channel_id=1, replica_groups=mesh['row'=4,'col'=8] {'col'}, dimensions={1}, use_global_device_ids=true | all-gather | bytes 294912 | tf_op jit(solution)/shard_map/all_gather | solution.py:132
  421.0 43.6 %while.57 = (s32[]{:T(128)}, f32[32,16,128]{2,1,0:T(8,128)S(1)}, f32[32,32,128]{2,1,0:T(8,128)S(1)}, s32[]{:T(128)}, s32[256]{0:T(256)S(1)}, /*index=5*/bf16[32,...) while((s32[]{:T(128)}, f32[32,16,128]{2,1,0:T(8,128)S(1)}, ...), condition=%wide.region_7.10_spmd.clone, body=%wide.region_6.9_spmd.clone.sunk | while | flops 71635120 | bytes 4466047 | solution.py:88
  466.9 68.4 %reduce-scatter.11.cloned.1.call-done = f32[32,512]{1,0:T(8,128)} async-done(((f32[32,2048]{1,0:T(8,128)}), f32[32,512]{1,0:T(8,128)}) %reduce-scatter.11.cloned.1.call-update) | async-done | bytes 65552 | tf_op jit(solution)/shard_map/reduce_scatter | solution.py:109
  535.2 65.6 %reduce-scatter.13.cloned.1.call-done = f32[32,512]{1,0:T(8,128)} async-done(((f32[32,4096]{1,0:T(8,128)}), f32[32,512]{1,0:T(8,128)}) %reduce-scatter.13.cloned.1.call-update) | async-done | bytes 65552 | tf_op jit(solution)/shard_map/reduce_scatter | solution.py:112
  601.9 40.3 %all-reduce = (f32[32,32]{1,0:T(8,128)S(1)}, f32[32,32]{1,0:T(8,128)S(1)}) all-reduce(f32[32,32]{1,0:T(8,128)S(1)} %fusion.140, f32[32,32]{1,0:T(8,128)S(1)} %convolution_bitcast_fusion.10), channel_id=1, replica_groups=mesh['row'=4,'col'=8] {'row','col'}, use_global_device_ids=true, to_apply=%region_13.17 | all-reduce | flops 2048 | bytes 16384 | tf_op jit(solution)/shard_map/psum | solution.py:126
  657.7 39.2 %psum.30 = f32[32,32]{1,0:T(8,128)S(1)} all-reduce(f32[32,32]{1,0:T(8,128)S(1)} %fusion.142), channel_id=1, replica_groups=mesh['row'=4,'col'=8] {'row','col'}, use_global_device_ids=true, to_apply=%region_14.20 | all-reduce | flops 1024 | bytes 8192 | tf_op jit(solution)/shard_map/psum | solution.py:126
  697.6 30.8 %all_gather.14 = bf16[32,4096]{1,0:T(8,128)(2,1)S(1)} all-gather(bf16[32,512]{1,0:T(8,128)(2,1)S(1)} %get-tuple-element.662), channel_id=1, replica_groups=mesh['row'=4,'col'=8] {'col'}, dimensions={1}, use_global_device_ids=true | all-gather | bytes 294912 | tf_op jit(solution)/shard_map/all_gather | solution.py:132
  728.3 5.9 all_gather.15
  734.4 43.7 %while.58 = (s32[]{:T(128)}, f32[32,16,128]{2,1,0:T(8,128)S(1)}, f32[32,32,128]{2,1,0:T(8,128)S(1)}, s32[]{:T(128)}, s32[256]{0:T(256)S(1)}, /*index=5*/bf16[32,...) while((s32[]{:T(128)}, f32[32,16,128]{2,1,0:T(8,128)S(1)}, ...), condition=%wide.region_16.22_spmd.clone, body=%wide.region_15.21_spmd.clone.sunk | while | flops 71635120 | bytes 4466047 | solution.py:88
  780.4 68.4 %reduce-scatter.15.cloned.1.call-done = f32[32,512]{1,0:T(8,128)} async-done(((f32[32,2048]{1,0:T(8,128)}), f32[32,512]{1,0:T(8,128)}) %reduce-scatter.15.cloned.1.call-update) | async-done | bytes 65552 | tf_op jit(solution)/shard_map/reduce_scatter | solution.py:109
  848.8 65.6 %reduce-scatter.17.cloned.1.call-done = f32[32,512]{1,0:T(8,128)} async-done(((f32[32,4096]{1,0:T(8,128)}), f32[32,512]{1,0:T(8,128)}) %reduce-scatter.17.cloned.1.call-update) | async-done | bytes 65552 | tf_op jit(solution)/shard_map/reduce_scatter | solution.py:112
  915.5 40.1 %psum.31 = f32[32,32]{1,0:T(8,128)S(1)} all-reduce(f32[32,32]{1,0:T(8,128)S(1)} %fusion.113), channel_id=1, replica_groups=mesh['row'=4,'col'=8] {'row','col'}, use_global_device_ids=true, to_apply=%region_19.25 | all-reduce | flops 1024 | bytes 8192 | tf_op jit(solution)/shard_map/psum | solution.py:141
  (456 shorter events, 197.0 us)
Async XLA Ops:
  7.2 191.4 %copy-start.1 = (s32[1,1,256]{2,1,0:T(1,128)S(1)}, s32[1,1,256]{2,1,0:T(1,128)}, u32[]{:S(2)}) copy-start(s32[1,1,256]{2,1,0:T(1,128)} %param.23) | copy-start | bytes 3076
  7.2 304.1 %reduce-scatter.19.cloned.1.call-start = ((), (), s32[]{:S(2)}) async-start(), calls=%async_computation.10 | async-start | bytes 1310720
  198.6 185.8 %copy-start = (f32[32,512]{1,0:T(8,128)S(1)}, f32[32,512]{1,0:T(8,128)}, u32[]{:S(2)}) copy-start(f32[32,512]{1,0:T(8,128)} %param.22) | copy-start | bytes 196612
  237.8 145.5 %reduce-scatter.21.cloned.1.call-start = ((), (), s32[]{:S(2)}) async-start(), calls=%async_computation.11 | async-start | bytes 2359296
  240.0 295.3 %reduce-scatter.11.cloned.1.call-start = ((), (), s32[]{:S(2)}) async-start(), calls=%async_computation.6 | async-start | bytes 327680 | tf_op jit(solution)/shard_map/reduce_scatter | solution.py:109
  465.4 135.4 %reduce-scatter.13.cloned.1.call-start = ((), (), s32[]{:S(2)}) async-start(), calls=%async_computation.7 | async-start | bytes 589824 | tf_op jit(solution)/shard_map/reduce_scatter | solution.py:112
  466.6 382.2 %reduce-scatter.15.cloned.1.call-start = ((), (), s32[]{:S(2)}) async-start(), calls=%async_computation.8 | async-start | bytes 327680 | tf_op jit(solution)/shard_map/reduce_scatter | solution.py:109
  778.9 135.5 %reduce-scatter.17.cloned.1.call-start = ((), (), s32[]{:S(2)}) async-start(), calls=%async_computation.9 | async-start | bytes 589824 | tf_op jit(solution)/shard_map/reduce_scatter | solution.py:112
Sparse Core Ops, SparseCore 0:
  238.0 73.3 reduce-scatter.18
  315.3 68.0 reduce-scatter.20
  465.5 69.6 reduce-scatter.10
  538.4 62.3 reduce-scatter.12
  779.0 69.6 reduce-scatter.14
  852.0 62.3 reduce-scatter.16
where the time goes:
time: 982 us; the launch traced here: 972 us
  waiting for transfers between devices  410 us (42%)
  other arithmetic  198 us (20%)
  blocking collectives  193 us (20%)
  matrix products  89.8 us (9%)
  local copies, waits for them, and re-layouts  63.8 us (6%)
  between operations  15 us (2%)
    dynamic_update_slice x16, other arithmetic, build_blocks(): lax.map(fill_group, (index_groups, value_groups))  160 us
    unnamed x8, waiting for transfers between devices  142 us
    reduce_scatter x2, waiting for transfers between devices, partial_sums(): lax.psum_scatter(row_total.reshape(query_rows, row_blocks * 128), 'row',...  137 us
    reduce_scatter x2, waiting for transfers between devices, partial_sums(): lax.psum_scatter(col_total.reshape(query_rows, col_blocks * 128), 'col',...  131 us
    psum x2, blocking collectives, residual_gram(): return symmetric(lax.psum(gram_matrix(current, current), ('row', 'col')))  79.5 us
    all_gather x2, blocking collectives, body(): lax.all_gather(scaled, 'col', axis=1, tiled=True)  61.7 us
    psum x1, blocking collectives, body(): lax.psum(gram_matrix(direction, applied), ('row', 'col'))  40.1 us
    dot_general x21, matrix products, group_turn(): jnp.einsum('sij,msj->msi', group_blocks, col_vecs, preferred_element_type...  30.2 us
  transfers between devices with their start and end apart: 6, of which 6 were waited for; matrix products, arithmetic and copies ran while one was open for 1% of the time, Pallas kernels for 0%

commit v1 on v0

v1 whole, which is shorter than its diff:
```python
import functools

import jax
import jax.numpy as jnp
from jax import lax
from jax.experimental import pallas as pl
from jax.experimental.pallas import tpu as pltpu
from jax.sharding import PartitionSpec as P

graph_weight = 0.95
GROUP = 16
VMEM_LIMIT = 48 * 1024 * 1024


def dot_plain(left, right, **kwargs):
    return lax.dot_general(
        left, right, (((1,), (0,)), ((), ())), preferred_element_type=jnp.float32, **kwargs
    )


def dot_across(left, right, **kwargs):
    return lax.dot_general(
        left, right, (((1,), (1,)), ((), ())), preferred_element_type=jnp.float32, **kwargs
    )


exact_plain = functools.partial(dot_plain, precision=lax.Precision.HIGHEST)
exact_across = functools.partial(dot_across, precision=lax.Precision.HIGHEST)


def build_kernel(
    col_blocks, spots_ref, live_ref, index_ref, value_ref, block_ref, row_ref, col_ref
):
    step = pl.program_id(0)
    live = live_ref[0]

    @pl.when(step == 0)
    def _():
        row_ref[...] = jnp.zeros_like(row_ref)
        col_ref[...] = jnp.zeros_like(col_ref)

    @pl.when(step * GROUP < live)
    def _():
        lanes = lax.broadcasted_iota(jnp.int32, (16, 128), 0).astype(jnp.float32)
        targets = [(lanes + 16.0 * part).astype(jnp.bfloat16) for part in range(8)]
        ones = jnp.ones((8, 128), jnp.bfloat16)
        zero = jnp.zeros((16, 128), jnp.bfloat16)
        row_sums = []
        col_sums = []
        for slot in range(GROUP):
            active = (step * GROUP + slot < live).astype(jnp.float32)
            index_f32 = index_ref[slot].astype(jnp.float32)
            value_f32 = value_ref[slot].astype(jnp.float32) * active
            sums = [zero] * 8
            for entry in range(16):
                index_row = jnp.broadcast_to(index_f32[entry : entry + 1], (16, 128)).astype(
                    jnp.bfloat16
                )
                value_row = jnp.broadcast_to(value_f32[entry : entry + 1], (16, 128)).astype(
                    jnp.bfloat16
                )
                for part in range(8):
                    sums[part] = sums[part] + jnp.where(
                        index_row == targets[part], value_row, zero
                    )
            block = jnp.concatenate(sums, axis=0)
            block_ref[slot] = block
            row_sums.append(dot_plain(ones, block))
            col_sums.append(dot_across(ones, block))
        for slot in range(GROUP):
            spot = spots_ref[step * GROUP + slot]
            row_ref[spot // col_blocks] += row_sums[slot]
            col_ref[spot % col_blocks] += col_sums[slot]


def build_blocks(spots, live, index_table, value_table, row_blocks, col_blocks):
    slots = index_table.shape[0]

    def clamp(step, spots_ref, live_ref):
        return (jnp.minimum(step, (live_ref[0] - 1) // GROUP), 0, 0)

    def whole(step, spots_ref, live_ref):
        return (0, 0, 0)

    return pl.pallas_call(
        functools.partial(build_kernel, col_blocks),
        grid_spec=pltpu.PrefetchScalarGridSpec(
            num_scalar_prefetch=2,
            grid=(slots // GROUP,),
            in_specs=[
                pl.BlockSpec((GROUP, 16, 128), clamp),
                pl.BlockSpec((GROUP, 16, 128), clamp),
            ],
            out_specs=[
                pl.BlockSpec((GROUP, 128, 128), clamp),
                pl.BlockSpec((row_blocks, 8, 128), whole),
                pl.BlockSpec((col_blocks, 8, 128), whole),
            ],
        ),
        out_shape=[
            jax.ShapeDtypeStruct((slots, 128, 128), jnp.bfloat16),
            jax.ShapeDtypeStruct((row_blocks, 8, 128), jnp.float32),
            jax.ShapeDtypeStruct((col_blocks, 8, 128), jnp.float32),
        ],
        compiler_params=pltpu.CompilerParams(vmem_limit_bytes=VMEM_LIMIT),
        name="build_blocks",
    )(spots, live, index_table, value_table)


def product_kernel(
    col_blocks,
    spots_ref,
    live_ref,
    block_ref,
    col_dir_ref,
    row_dir_ref,
    row_out_ref,
    col_out_ref,
    row_ref,
    col_ref,
):
    step = pl.program_id(0)
    live = live_ref[0]

    @pl.when(step == 0)
    def _():
        row_ref[...] = jnp.zeros_like(row_ref)
        col_ref[...] = jnp.zeros_like(col_ref)

    @pl.when(step * GROUP < live)
    def _():
        row_sums = []
        col_sums = []
        for slot in range(GROUP):
            spot = spots_ref[step * GROUP + slot]
            block = block_ref[slot]
            row_sums.append(dot_plain(col_dir_ref[spot % col_blocks], block))
            col_sums.append(dot_across(row_dir_ref[spot // col_blocks], block))
        for slot in range(GROUP):
            spot = spots_ref[step * GROUP + slot]
            row_ref[spot // col_blocks] += row_sums[slot]
            col_ref[spot % col_blocks] += col_sums[slot]

    @pl.when(step == pl.num_programs(0) - 1)
    def _():
        row_out_ref[...] = row_ref[...].astype(row_out_ref.dtype)
        col_out_ref[...] = col_ref[...].astype(col_out_ref.dtype)


def block_products(spots, live, blocks, col_dirs, row_dirs):
    slots = blocks.shape[0]

    def clamp(step, spots_ref, live_ref):
        return (jnp.minimum(step, (live_ref[0] - 1) // GROUP), 0, 0)

    def whole(step, spots_ref, live_ref):
        return (0, 0, 0)

    return pl.pallas_call(
        functools.partial(product_kernel, col_dirs.shape[0]),
        grid_spec=pltpu.PrefetchScalarGridSpec(
            num_scalar_prefetch=2,
            grid=(slots // GROUP,),
            in_specs=[
                pl.BlockSpec((GROUP, 128, 128), clamp),
                pl.BlockSpec(col_dirs.shape, whole),
                pl.BlockSpec(row_dirs.shape, whole),
            ],
            out_specs=[
                pl.BlockSpec(row_dirs.shape, whole),
                pl.BlockSpec(col_dirs.shape, whole),
            ],
            scratch_shapes=[
                pltpu.VMEM(row_dirs.shape, jnp.float32),
                pltpu.VMEM(col_dirs.shape, jnp.float32),
            ],
        ),
        out_shape=[
            jax.ShapeDtypeStruct(row_dirs.shape, jnp.bfloat16),
            jax.ShapeDtypeStruct(col_dirs.shape, jnp.bfloat16),
        ],
        compiler_params=pltpu.CompilerParams(vmem_limit_bytes=VMEM_LIMIT),
        name="block_products",
    )(spots, live, blocks, col_dirs, row_dirs)


def start_kernel(row_ref, col_ref, query_ref, scaling_ref, scaled_ref):
    degree = 1.0 + 0.5 * (jnp.sum(row_ref[...], axis=0) + jnp.sum(col_ref[...], axis=0))
    scaling = 1.0 / jnp.sqrt(degree)
    scaling_ref[...] = scaling
    for part in range(scaling.shape[0]):
        scaled_ref[part] = (
            scaling[part : part + 1] * query_ref[:, part * 128 : part * 128 + 128]
        ).astype(jnp.bfloat16)


def summed(ref, part):
    total = ref[0, part].astype(jnp.float32)
    for other in range(1, ref.shape[0]):
        total = total + ref[other, part].astype(jnp.float32)
    return total


def middle_kernel(row_ref, col_ref, scaling_ref, first_ref, scaled_ref):
    for part in range(scaling_ref.shape[0]):
        scaling = scaling_ref[part : part + 1]
        first = scaling * (0.5 * (summed(row_ref, part) + summed(col_ref, part)))
        first_ref[part] = first
        scaled_ref[part] = (scaling * first).astype(jnp.bfloat16)


def gram_kernel(row_ref, col_ref, scaling_ref, query_ref, first_ref, second_ref, gram_ref):
    per_seg = scaling_ref.shape[0]
    query_query = jnp.zeros((32, 32), jnp.float32)
    query_first = query_query
    first_first = query_query
    first_second = query_query
    for part in range(per_seg):
        scaling = scaling_ref[part : part + 1]
        second = scaling * (0.5 * (summed(row_ref, part) + summed(col_ref, part)))
        second_ref[part] = second
        first = first_ref[part]
        query = query_ref[:, part * 128 : part * 128 + 128]
        query_query += exact_across(query, query)
        query_first += exact_across(query, first)
        first_first += exact_across(first, first)
        first_second += exact_across(first, second)
    gram_ref[...] = jnp.concatenate([query_query, query_first, first_first, first_second], axis=1)


def tall(flat):
    rest = flat.shape[1] - flat.shape[0]
    return jnp.concatenate([flat, jnp.zeros((rest, flat.shape[1]), flat.dtype)], axis=0)


def flipped(flat):
    return tall(flat).T[: flat.shape[0]]


def times(left, right):
    return exact_plain(left, tall(right))


def beside(left, right):
    return left + pltpu.roll(right, left.shape[0], 1)


def stacked(upper, lower):
    rest = jnp.zeros((upper.shape[1] - 2 * upper.shape[0], upper.shape[1]), upper.dtype)
    return jnp.concatenate([upper, lower, rest], axis=0)


def sandwich(rows, middle):
    return exact_across(exact_plain(rows, middle), tall(rows))


def symmetric(flat):
    return 0.5 * (flat + flipped(flat))


def window(flat, place):
    size = flat.shape[0]
    if place:
        flat = pltpu.roll(flat, flat.shape[1] - place * size, 1)
    lanes = lax.broadcasted_iota(jnp.int32, flat.shape, 1)
    return jnp.where(lanes < size, flat, 0.0)


def solve_many(pairs):
    size = pairs[0][0].shape[0]
    systems = [matrix + pltpu.roll(side, size, 1) for matrix, side in pairs]
    sublanes = lax.broadcasted_iota(jnp.int32, systems[0].shape, 0)
    for pivot in range(size):
        updated = []
        for system in systems:
            column = system[:, pivot : pivot + 1]
            row = system[pivot : pivot + 1, :] / column[pivot : pivot + 1, :]
            updated.append(jnp.where(sublanes == pivot, row, system - column * row))
        systems = updated
    return [window(system, 1) for system in systems]


def close_kernel(gram_ref, query_ref, first_ref, second_ref, solution_ref, residual_ref):
    size = query_ref.shape[0]
    weight = graph_weight
    total = gram_ref[0]
    for other in range(1, gram_ref.shape[0]):
        total = total + gram_ref[other]
    g00 = symmetric(window(total, 0))
    g01 = window(total, 1)
    g11 = symmetric(window(total, 2))
    g12 = window(total, 3)
    eye = (
        lax.broadcasted_iota(jnp.int32, total.shape, 0)
        == lax.broadcasted_iota(jnp.int32, total.shape, 1)
    ).astype(jnp.float32)
    curve = symmetric(g00 - weight * g01)
    steps, inverse = solve_many([(curve, g00), (g00, eye)])
    steps_t = flipped(steps)
    plain_gram = stacked(beside(g00, g01), beside(flipped(g01), g11))
    through_gram = stacked(beside(g01, g11), beside(g11, g12))
    after_first = beside(eye - steps_t, weight * steps_t)
    new_gram = symmetric(sandwich(after_first, plain_gram))
    mixing = times(inverse, new_gram)
    direction = after_first + flipped(mixing)
    curve = symmetric(sandwich(direction, plain_gram - weight * through_gram))
    (steps,) = solve_many([(curve, new_gram)])
    steps_t2 = flipped(steps)
    applied = direction - weight * pltpu.roll(direction, size, 1)
    solution_rows = exact_plain(beside(eye, steps_t2), stacked(steps_t, direction))
    residual_rows = exact_plain(beside(eye, -steps_t2), stacked(after_first, applied))
    rows = jnp.concatenate([solution_rows, residual_rows], axis=0)
    for part in range(first_ref.shape[0]):
        lanes = slice(part * 128, part * 128 + 128)
        basis = jnp.concatenate(
            [query_ref[:, lanes], first_ref[part], second_ref[part], jnp.zeros_like(eye)], axis=0
        )
        values = exact_plain(rows, basis)
        solution_ref[:, lanes] = values[:size]
        residual_ref[:, lanes] = values[size:]


def exchange(parts, axis):
    return lax.all_to_all(parts, axis, 0, 0, tiled=True)


def spread(piece, axis):
    count = lax.axis_size(axis)
    return exchange(jnp.broadcast_to(piece[None], (count,) + piece.shape), axis)


def simple_call(kernel, shapes, name, *operands):
    return pl.pallas_call(
        kernel,
        out_shape=shapes,
        compiler_params=pltpu.CompilerParams(vmem_limit_bytes=VMEM_LIMIT),
        name=name,
    )(*operands)


def body(queries, block_spots, live_blocks, neighbor_cols, neighbor_sims):
    row_count = lax.axis_size("row")
    col_count = lax.axis_size("col")
    query_rows, seg_len = queries.shape
    per_seg = seg_len // 128
    row_blocks = row_count * per_seg
    col_blocks = col_count * per_seg
    spots = block_spots[0, 0]
    live = live_blocks[0]
    piece = (per_seg, query_rows, 128)
    wide = jax.ShapeDtypeStruct(piece, jnp.float32)
    narrow = jax.ShapeDtypeStruct(piece, jnp.bfloat16)

    blocks, row_sums, col_sums = build_blocks(
        spots, live, neighbor_cols[0, 0], neighbor_sims[0, 0], row_blocks, col_blocks
    )
    row_parts = exchange(row_sums[:, 0].reshape(row_count, per_seg, 128), "row")
    col_parts = exchange(col_sums[:, 0].reshape(col_count, per_seg, 128), "col")
    scaling, scaled = simple_call(
        start_kernel,
        [jax.ShapeDtypeStruct((per_seg, 128), jnp.float32), narrow],
        "start",
        row_parts,
        col_parts,
        queries,
    )

    def product(vectors):
        col_dirs = spread(vectors, "col").reshape(col_blocks, query_rows, 128)
        row_dirs = spread(vectors, "row").reshape(row_blocks, query_rows, 128)
        row_total, col_total = block_products(spots, live, blocks, col_dirs, row_dirs)
        return (
            exchange(row_total.reshape((row_count,) + piece), "row"),
            exchange(col_total.reshape((col_count,) + piece), "col"),
        )

    row_parts, col_parts = product(scaled)
    first, scaled = simple_call(
        middle_kernel, [wide, narrow], "middle", row_parts, col_parts, scaling
    )
    row_parts, col_parts = product(scaled)
    second, grams = simple_call(
        gram_kernel,
        [wide, jax.ShapeDtypeStruct((query_rows, 4 * query_rows), jnp.float32)],
        "grams",
        row_parts,
        col_parts,
        scaling,
        queries,
        first,
    )
    all_grams = spread(grams, ("row", "col"))
    flat = jax.ShapeDtypeStruct(queries.shape, jnp.float32)
    return tuple(
        simple_call(close_kernel, [flat, flat], "close", all_grams, queries, first, second)
    )


def solution(mesh):
    placed = (
        P(None, ("row", "col")),
        P("row", "col", None),
        P("row", "col"),
        P("row", "col", None, None, None),
        P("row", "col", None, None, None),
    )
    return jax.shard_map(
        body,
        mesh=mesh,
        in_specs=placed,
        out_specs=(P(None, ("row", "col")), P(None, ("row", "col"))),
        check_vma=False,
    )
```

time: 982 us -> 175 us (0.18)
  waiting for transfers between devices: 410 us -> 3.8 us
  other arithmetic: 198 us -> 0 us
  matrix products: 89.8 us -> 0 us
  blocking collectives: 193 us -> 131 us
  local copies, waits for them, and re-layouts: 63.8 us -> 5.84 us
  Pallas kernels: 0 us -> 25.5 us
  between operations: 15 us -> 1.39 us
    reduce_scatter x4 -> x0, waiting for transfers between devices: 268 us -> none  [the longest x2 137 us: partial_sums(): lax.psum_scatter(row_total.reshape(query_rows, row_blocks * 128), 'row',...]
    dynamic_update_slice x16 -> x0, other arithmetic: 160 us -> none  [build_blocks(): lax.map(fill_group, (index_groups, value_groups))]
    unnamed x8 -> x0, waiting for transfers between devices: 142 us -> none
    all_to_all x0 -> x10, blocking collectives: none -> 131 us  [exchange(): return lax.all_to_all(parts, axis, 0, 0, tiled=True)]
    psum x3 -> x0, blocking collectives: 120 us -> none  [the longest x2 79.5 us: residual_gram(): return symmetric(lax.psum(gram_matrix(current, current), ('row', 'col')))]
    dot_general x93 -> x0, matrix products: 88.7 us -> none  [the longest x21 30.2 us: group_turn(): jnp.einsum('sij,msj->msi', group_blocks, col_vecs, preferred_element_type...]
    all_gather x4 -> x0, blocking collectives: 73 us -> none  [the longest x2 61.7 us: body(): lax.all_gather(scaled, 'col', axis=1, tiled=True)]
    dynamic_slice x64 -> x0, local copies, waits for them, and re-layouts: 29.2 us -> none  [build_blocks(): lax.map(fill_group, (index_groups, value_groups))]
  transfers between devices with their start and end apart: 6 -> 1, of which waited for: 6 -> 1; matrix products, arithmetic and copies ran while one was open for 1% -> 0% of each run, Pallas kernels for 0% -> 0%
where the time goes in v1:
time: 175 us
  blocking collectives  131 us (75%)
  Pallas kernels  25.5 us (15%)
  starting transfers between devices  7.59 us (4%)
  local copies, waits for them, and re-layouts  5.84 us (3%)
  waiting for transfers between devices  3.8 us (2%)
    all_to_all x10, blocking collectives, exchange(): return lax.all_to_all(parts, axis, 0, 0, tiled=True)  131 us
    pallas_call x2, Pallas kernels, block_products(): pl.pallas_call(functools.partial(product_kernel, col_dirs.shape[0]), grid...  9.73 us
    pallas_call x4, Pallas kernels, simple_call(): pl.pallas_call(kernel, out_shape=shapes, compiler_params=pltpu.CompilerPa...  9.06 us
    all_to_all x1, starting transfers between devices, exchange(): return lax.all_to_all(parts, axis, 0, 0, tiled=True)  7.59 us
    pallas_call x1, Pallas kernels, build_blocks(): pl.pallas_call(functools.partial(build_kernel, col_blocks), grid_spec=plt...  6.66 us
    unnamed x14, local copies, waits for them, and re-layouts  5.02 us
    all_to_all x1, waiting for transfers between devices, exchange(): return lax.all_to_all(parts, axis, 0, 0, tiled=True)  3.8 us
  transfers between devices with their start and end apart: 1, of which 1 were waited for; matrix products, arithmetic and copies ran while one was open for 0% of the time, Pallas kernels for 0%

profile of v1, /device:TPU:0, one launch (start us, length us, event | category | flops | bytes accessed | tf_op | source)
XLA Modules:
  0.0 175.0 jit_solution(16284099415058313785)
XLA Ops:
  0.6 0.0 copy-start.6
  1.3 0.0 copy-start
  1.3 1.6 copy-done
  2.9 0.0 copy-start.1
  2.9 1.2 copy-done.1
  4.1 0.0 copy-start.4
  4.1 0.7 copy-done.4
  4.8 6.7 %build_blocks.1 = (bf16[256,128,128]{2,1,0:T(8,128)(2,1)}, f32[16,8,128]{2,1,0:T(8,128)S(1)}, f32[32,8,128]{2,1,0:T(8,128)S(1)}) custom-call(s32[256]{0:T(256)S(1)} %bitcast.27, s32[1]{0:T(128)} %bitcast.14.live_ref, s32[256,16,128]{2,1,0:T(8,128)S(1)} %bitcast.17, bf16[256,16,128]{2,1,0:T(8,128)(2,1)S(1)} %bitcast.20), custom_call_target="tpu_custom_call" | custom-call | tf_op jit(solution)/shard_map/build_blocks/pallas_call | solution.py:85
  11.5 0.6 slice.6
  12.1 7.6 %all-to-all-start = ((f32[4,4,128]{2,1,0:T(4,128)}), f32[4,4,128]{2,1,0:T(4,128)S(1)}, u32[]{:S(2)}, u32[]{:S(2)}) async-start(f32[4,4,128]{2,1,0:T(4,128)} %bitcast.4), calls=%async_computation | async-start | bytes 16384 | tf_op jit(solution)/shard_map/all_to_all | solution.py:324
  19.7 3.8 %all-to-all-done.row_ref = f32[4,4,128]{2,1,0:T(4,128)S(1)} async-done(((f32[4,4,128]{2,1,0:T(4,128)}), f32[4,4,128]{2,1,0:T(4,128)S(1)}, u32[]{:S(2)}, u32[]{:S(2)}) %all-to-all-start) | async-done | bytes 8224 | tf_op jit(solution)/shard_map/all_to_all | solution.py:324
  23.5 21.4 %all_to_all.55.col_ref = f32[8,4,128]{2,1,0:T(4,128)S(1)} all-to-all(f32[8,4,128]{2,1,0:T(4,128)S(1)} %bitcast.30), channel_id=1, replica_groups=mesh['row'=4,'col'=8] {'col'}, dimensions={0} | all-to-all | bytes 32768 | tf_op jit(solution)/shard_map/all_to_all | solution.py:324
  44.9 0.0 copy-start.2
  44.9 0.8 copy-done.2
  45.8 7.0 %all_to_all.56 = bf16[4,4,32,128]{3,2,1,0:T(8,128)(2,1)S(1)} all-to-all(bf16[4,4,32,128]{3,2,1,0:T(8,128)(2,1)S(1)} %broadcast_in_dim.11), channel_id=1, replica_groups=mesh['row'=4,'col'=8] {'row'}, dimensions={0} | all-to-all | bytes 262144 | tf_op jit(solution)/shard_map/all_to_all | solution.py:324
  52.9 11.2 %all_to_all.57 = bf16[8,4,32,128]{3,2,1,0:T(8,128)(2,1)S(1)} all-to-all(bf16[8,4,32,128]{3,2,1,0:T(8,128)(2,1)S(1)} %broadcast_in_dim.10), channel_id=1, replica_groups=mesh['row'=4,'col'=8] {'col'}, dimensions={0} | all-to-all | bytes 524288 | tf_op jit(solution)/shard_map/all_to_all | solution.py:324
  64.1 0.7 copy-done.5
  64.8 4.9 %block_products.2 = (bf16[16,32,128]{2,1,0:T(8,128)(2,1)S(1)}, bf16[32,32,128]{2,1,0:T(8,128)(2,1)S(1)}) custom-call(s32[256]{0:T(256)S(1)} %bitcast.28, s32[1]{0:T(128)} %bitcast.15.live_ref, bf16[256,128,128]{2,1,0:T(8,128)(2,1)} %get-tuple-element.15.block_ref, bf16[32,32,128]{2,1,0:T(8,128)(2,1)S(1)} %bitcast.19, bf16[16,32,128]{2,1,0:T(8,128)(2,1)S(1)} %bitcast.22), custom_call_target="tpu_custom_call" | custom-call | tf_op jit(solution)/shard_map/block_products/pallas_call | solution.py:159
  69.7 9.0 %all_to_all.58.row_ref = bf16[4,4,32,128]{3,2,1,0:T(8,128)(2,1)S(1)} all-to-all(bf16[4,4,32,128]{3,2,1,0:T(8,128)(2,1)S(1)} %bitcast.26), channel_id=1, replica_groups=mesh['row'=4,'col'=8] {'row'}, dimensions={0} | all-to-all | bytes 262144 | tf_op jit(solution)/shard_map/all_to_all | solution.py:324
  78.7 17.6 %all_to_all.59.col_ref = bf16[8,4,32,128]{3,2,1,0:T(8,128)(2,1)S(1)} all-to-all(bf16[8,4,32,128]{3,2,1,0:T(8,128)(2,1)S(1)} %bitcast.24), channel_id=1, replica_groups=mesh['row'=4,'col'=8] {'col'}, dimensions={0} | all-to-all | bytes 524288 | tf_op jit(solution)/shard_map/all_to_all | solution.py:324
  96.3 0.1 middle.1
  96.4 7.0 %all_to_all.60 = bf16[4,4,32,128]{3,2,1,0:T(8,128)(2,1)S(1)} all-to-all(bf16[4,4,32,128]{3,2,1,0:T(8,128)(2,1)S(1)} %broadcast_in_dim.13), channel_id=1, replica_groups=mesh['row'=4,'col'=8] {'row'}, dimensions={0} | all-to-all | bytes 262144 | tf_op jit(solution)/shard_map/all_to_all | solution.py:324
  103.4 11.9 %all_to_all.61 = bf16[8,4,32,128]{3,2,1,0:T(8,128)(2,1)S(1)} all-to-all(bf16[8,4,32,128]{3,2,1,0:T(8,128)(2,1)S(1)} %broadcast_in_dim.12), channel_id=1, replica_groups=mesh['row'=4,'col'=8] {'col'}, dimensions={0} | all-to-all | bytes 524288 | tf_op jit(solution)/shard_map/all_to_all | solution.py:324
  115.4 0.0 copy-done.6
  115.4 4.9 %block_products.3 = (bf16[16,32,128]{2,1,0:T(8,128)(2,1)S(1)}, bf16[32,32,128]{2,1,0:T(8,128)(2,1)S(1)}) custom-call(s32[256]{0:T(256)S(1)} %bitcast.29, s32[1]{0:T(128)} %bitcast.16.live_ref, bf16[256,128,128]{2,1,0:T(8,128)(2,1)} %get-tuple-element.15.block_ref, bf16[32,32,128]{2,1,0:T(8,128)(2,1)S(1)} %bitcast.18, bf16[16,32,128]{2,1,0:T(8,128)(2,1)S(1)} %bitcast.21), custom_call_target="tpu_custom_call" | custom-call | tf_op jit(solution)/shard_map/block_products/pallas_call | solution.py:159
  120.2 9.0 %all_to_all.62.row_ref = bf16[4,4,32,128]{3,2,1,0:T(8,128)(2,1)S(1)} all-to-all(bf16[4,4,32,128]{3,2,1,0:T(8,128)(2,1)S(1)} %bitcast.25), channel_id=1, replica_groups=mesh['row'=4,'col'=8] {'row'}, dimensions={0} | all-to-all | bytes 262144 | tf_op jit(solution)/shard_map/all_to_all | solution.py:324
  129.2 17.6 %all_to_all.63.col_ref = bf16[8,4,32,128]{3,2,1,0:T(8,128)(2,1)S(1)} all-to-all(bf16[8,4,32,128]{3,2,1,0:T(8,128)(2,1)S(1)} %bitcast.23), channel_id=1, replica_groups=mesh['row'=4,'col'=8] {'col'}, dimensions={0} | all-to-all | bytes 524288 | tf_op jit(solution)/shard_map/all_to_all | solution.py:324
  146.8 0.0 copy-done.3
  146.8 0.6 grams.1
  147.4 0.1 broadcast_in_dim.14
  147.5 19.1 %all_to_all.64.gram_ref = f32[32,32,128]{2,1,0:T(8,128)S(1)} all-to-all(f32[32,32,128]{2,1,0:T(8,128)S(1)} %broadcast_in_dim.14), channel_id=1, replica_groups=mesh['row'=4,'col'=8] {'row','col'}, dimensions={0} | all-to-all | bytes 1048576 | tf_op jit(solution)/shard_map/all_to_all | solution.py:324
  166.6 8.4 %close.1 = (f32[32,512]{1,0:T(8,128)}, f32[32,512]{1,0:T(8,128)}) custom-call(f32[32,32,128]{2,1,0:T(8,128)S(1)} %all_to_all.64.gram_ref, f32[32,512]{1,0:T(8,128)S(1)} %copy-done.3, f32[4,32,128]{2,1,0:T(8,128)S(1)} %get-tuple-element.25.first_ref, f32[4,32,128]{2,1,0:T(8,128)S(1)} %get-tuple-element.27.second_ref), custom_call_target="tpu_custom_call" | custom-call | tf_op jit(solution)/shard_map/close/pallas_call | solution.py:333
  (8 shorter events, 0.2 us)
Async XLA Ops:
  0.6 114.7 %copy-start.6 = (s32[1,1,256]{2,1,0:T(1,128)S(1)}, s32[1,1,256]{2,1,0:T(1,128)}, u32[]{:S(2)}) copy-start(s32[1,1,256]{2,1,0:T(1,128)} %param.6) | copy-start | bytes 3076
  1.3 1.6 copy-start
  2.9 1.2 copy-start.1
  4.1 0.7 copy-start.4
  12.1 11.4 %all-to-all-start = ((f32[4,4,128]{2,1,0:T(4,128)}), f32[4,4,128]{2,1,0:T(4,128)S(1)}, u32[]{:S(2)}, u32[]{:S(2)}) async-start(f32[4,4,128]{2,1,0:T(4,128)} %bitcast.4), calls=%async_computation | async-start | bytes 16384 | tf_op jit(solution)/shard_map/all_to_all | solution.py:324
  44.9 0.8 copy-start.2
  64.1 0.7 copy-start.5
  64.8 82.0 %copy-start.3 = (f32[32,512]{1,0:T(8,128)S(1)}, f32[32,512]{1,0:T(8,128)}, u32[]{:S(2)}) copy-start(f32[32,512]{1,0:T(8,128)} %query_ref.5) | copy-start | bytes 196612

commit v2 on v1

v2 whole, which is shorter than its diff:
```python
import functools

import jax
import jax.numpy as jnp
from jax import lax
from jax.experimental import pallas as pl
from jax.experimental.pallas import tpu as pltpu
from jax.sharding import PartitionSpec as P

graph_weight = 0.95
GROUP = 16
VMEM_LIMIT = 60 * 1024 * 1024


def dot_plain(left, right, **kwargs):
    return lax.dot_general(
        left, right, (((1,), (0,)), ((), ())), preferred_element_type=jnp.float32, **kwargs
    )


def dot_across(left, right, **kwargs):
    return lax.dot_general(
        left, right, (((1,), (1,)), ((), ())), preferred_element_type=jnp.float32, **kwargs
    )


exact_plain = functools.partial(dot_plain, precision=lax.Precision.HIGHEST)
exact_across = functools.partial(dot_across, precision=lax.Precision.HIGHEST)


def place_of(spots_ref, slot, col_blocks):
    spot = spots_ref[slot]
    return spot // col_blocks, spot % col_blocks


def build_kernel(row_count, col_count, per_seg, spots_ref, facts_ref, index_ref, value_ref, *refs):
    block_ref = refs[0]
    row_outs = refs[1 : 1 + row_count]
    col_outs = refs[1 + row_count : 1 + row_count + col_count]
    row_ref, col_ref = refs[1 + row_count + col_count :]
    col_blocks = col_count * per_seg
    step = pl.program_id(0)
    live = facts_ref[0]

    @pl.when(step == 0)
    def _():
        row_ref[...] = jnp.zeros_like(row_ref)
        col_ref[...] = jnp.zeros_like(col_ref)

    @pl.when(step * GROUP < live)
    def _():
        lanes = lax.broadcasted_iota(jnp.int32, (16, 128), 0).astype(jnp.float32)
        targets = [(lanes + 16.0 * part).astype(jnp.bfloat16) for part in range(8)]
        ones = jnp.ones((8, 128), jnp.bfloat16)
        zero = jnp.zeros((16, 128), jnp.bfloat16)
        row_sums = []
        col_sums = []
        for slot in range(GROUP):
            active = (step * GROUP + slot < live).astype(jnp.float32)
            index_f32 = index_ref[slot].astype(jnp.float32)
            value_f32 = value_ref[slot].astype(jnp.float32) * active
            sums = [zero] * 8
            for entry in range(16):
                index_row = jnp.broadcast_to(index_f32[entry : entry + 1], (16, 128)).astype(
                    jnp.bfloat16
                )
                value_row = jnp.broadcast_to(value_f32[entry : entry + 1], (16, 128)).astype(
                    jnp.bfloat16
                )
                for part in range(8):
                    sums[part] = sums[part] + jnp.where(
                        index_row == targets[part], value_row, zero
                    )
            block = jnp.concatenate(sums, axis=0)
            block_ref[slot] = block
            row_sums.append(dot_plain(ones, block))
            col_sums.append(dot_across(ones, block))
        for slot in range(GROUP):
            row_block, col_block = place_of(spots_ref, step * GROUP + slot, col_blocks)
            row_ref[row_block] += row_sums[slot]
            col_ref[col_block] += col_sums[slot]

    @pl.when(step == pl.num_programs(0) - 1)
    def _():
        for outs, total_ref, mine in ((row_outs, row_ref, facts_ref[1]), (col_outs, col_ref, facts_ref[2])):
            for ahead, out in enumerate(outs):
                first = lax.rem(mine + ahead, len(outs)) * per_seg
                for part in range(per_seg):
                    out[part : part + 1] = total_ref[first + part][:1]


def clamp_group(step, spots_ref, facts_ref):
    return (jnp.minimum(step, (facts_ref[0] - 1) // GROUP), 0, 0)


def whole_array(rank):
    return lambda step, spots_ref, facts_ref: (0,) * rank


def build_blocks(spots, facts, index_table, value_table, row_count, col_count, per_seg):
    slots = index_table.shape[0]
    devices = row_count + col_count
    return pl.pallas_call(
        functools.partial(build_kernel, row_count, col_count, per_seg),
        grid_spec=pltpu.PrefetchScalarGridSpec(
            num_scalar_prefetch=2,
            grid=(slots // GROUP,),
            in_specs=[
                pl.BlockSpec((GROUP, 16, 128), clamp_group),
                pl.BlockSpec((GROUP, 16, 128), clamp_group),
            ],
            out_specs=[pl.BlockSpec((GROUP, 128, 128), clamp_group)]
            + [pl.BlockSpec((per_seg, 128), whole_array(2))] * devices,
            scratch_shapes=[
                pltpu.VMEM((row_count * per_seg, 8, 128), jnp.float32),
                pltpu.VMEM((col_count * per_seg, 8, 128), jnp.float32),
            ],
        ),
        out_shape=[jax.ShapeDtypeStruct((slots, 128, 128), jnp.bfloat16)]
        + [jax.ShapeDtypeStruct((per_seg, 128), jnp.float32)] * devices,
        compiler_params=pltpu.CompilerParams(vmem_limit_bytes=VMEM_LIMIT),
        name="build_blocks",
    )(spots, facts, index_table, value_table)


def product_kernel(row_count, col_count, with_gram, spots_ref, facts_ref, block_ref, *refs):
    refs = list(refs)

    def take(count):
        taken = refs[:count]
        del refs[:count]
        return taken

    row_pieces = take(row_count)
    col_pieces = take(col_count)
    gram_in = take(1) if with_gram else None
    row_outs = take(row_count)
    col_outs = take(col_count)
    gram_out = take(1) if with_gram else None
    row_dir_ref, col_dir_ref, row_ref, col_ref = refs
    per_seg = row_pieces[0].shape[0]
    col_blocks = col_count * per_seg
    step = pl.program_id(0)
    live = facts_ref[0]

    @pl.when(step == 0)
    def _():
        row_ref[...] = jnp.zeros_like(row_ref)
        col_ref[...] = jnp.zeros_like(col_ref)
        for pieces, dir_ref, mine in (
            (row_pieces, row_dir_ref, facts_ref[1]),
            (col_pieces, col_dir_ref, facts_ref[2]),
        ):
            for behind, piece in enumerate(pieces):
                first = lax.rem(mine + (len(pieces) - behind), len(pieces)) * per_seg
                for part in range(per_seg):
                    dir_ref[first + part] = piece[part]

    @pl.when(step * GROUP < live)
    def _():
        row_sums = []
        col_sums = []
        for slot in range(GROUP):
            row_block, col_block = place_of(spots_ref, step * GROUP + slot, col_blocks)
            block = block_ref[slot]
            row_sums.append(dot_plain(col_dir_ref[col_block], block))
            col_sums.append(dot_across(row_dir_ref[row_block], block))
        for slot in range(GROUP):
            row_block, col_block = place_of(spots_ref, step * GROUP + slot, col_blocks)
            row_ref[row_block] += row_sums[slot]
            col_ref[col_block] += col_sums[slot]

    @pl.when(step == pl.num_programs(0) - 1)
    def _():
        for outs, total_ref, mine in (
            (row_outs, row_ref, facts_ref[1]),
            (col_outs, col_ref, facts_ref[2]),
        ):
            for ahead, out in enumerate(outs):
                first = lax.rem(mine + ahead, len(outs)) * per_seg
                for part in range(per_seg):
                    out[part] = total_ref[first + part].astype(out.dtype)
        if with_gram:
            size = row_ref.shape[1]

            def add_segment(segment, total):
                for part in range(per_seg):
                    col_block = segment * per_seg + part
                    values = col_ref[col_block]
                    high = values.astype(jnp.bfloat16)
                    low = (values - high.astype(jnp.float32)).astype(jnp.bfloat16)
                    total += dot_across(
                        jnp.concatenate([high, low], axis=0), tall(col_dir_ref[col_block])
                    )
                return total

            total = lax.fori_loop(
                0, col_count, add_segment, jnp.zeros((2 * size, 128), jnp.float32)
            )
            gram_out[0][...] = gram_in[0][...] + pltpu.roll(total[:size] + total[size:], 3 * size, 1)


def block_products(spots, facts, blocks, row_pieces, col_pieces, gram=None):
    slots = blocks.shape[0]
    piece = row_pieces[0]
    per_seg, rows, lanes = piece.shape
    devices = len(row_pieces) + len(col_pieces)
    grams = [] if gram is None else [gram]
    piece_specs = [pl.BlockSpec(piece.shape, whole_array(3))] * devices
    gram_specs = [pl.BlockSpec(item.shape, whole_array(2)) for item in grams]
    row_shape = (len(row_pieces) * per_seg, rows, lanes)
    col_shape = (len(col_pieces) * per_seg, rows, lanes)
    return pl.pallas_call(
        functools.partial(product_kernel, len(row_pieces), len(col_pieces), gram is not None),
        grid_spec=pltpu.PrefetchScalarGridSpec(
            num_scalar_prefetch=2,
            grid=(slots // GROUP,),
            in_specs=[pl.BlockSpec((GROUP, 128, 128), clamp_group)] + piece_specs + gram_specs,
            out_specs=piece_specs + gram_specs,
            scratch_shapes=[
                pltpu.VMEM(row_shape, jnp.bfloat16),
                pltpu.VMEM(col_shape, jnp.bfloat16),
                pltpu.VMEM(row_shape, jnp.float32),
                pltpu.VMEM(col_shape, jnp.float32),
            ],
        ),
        out_shape=[jax.ShapeDtypeStruct(piece.shape, jnp.bfloat16)] * devices
        + [jax.ShapeDtypeStruct(item.shape, jnp.float32) for item in grams],
        compiler_params=pltpu.CompilerParams(vmem_limit_bytes=VMEM_LIMIT),
        name="block_products",
    )(spots, facts, blocks, *row_pieces, *col_pieces, *grams)


def total_of(refs):
    total = refs[0][...].astype(jnp.float32)
    for ref in refs[1:]:
        total = total + ref[...].astype(jnp.float32)
    return total


def start_kernel(*refs):
    *degree_refs, query_ref, scaling_ref, scaled_ref = refs
    degree = 1.0 + 0.5 * total_of(degree_refs)
    scaling = 1.0 / jnp.sqrt(degree)
    scaling_ref[...] = scaling
    for part in range(scaling.shape[0]):
        scaled_ref[part] = (
            scaling[part : part + 1] * query_ref[:, part * 128 : part * 128 + 128]
        ).astype(jnp.bfloat16)


def scaled_sum(refs, scaling_ref, part):
    scaling = scaling_ref[part : part + 1]
    return scaling * (0.5 * total_of([ref.at[part] for ref in refs]))


def middle_kernel(*refs):
    *part_refs, scaling_ref, query_ref, first_ref, scaled_ref, gram_ref = refs
    size = query_ref.shape[0]
    pair_gram = jnp.zeros((2 * size, 128), jnp.float32)
    for part in range(scaling_ref.shape[0]):
        first = scaled_sum(part_refs, scaling_ref, part)
        first_ref[part] = first
        scaled_ref[part] = (scaling_ref[part : part + 1] * first).astype(jnp.bfloat16)
        pair = jnp.concatenate(
            [query_ref[:, part * 128 : part * 128 + 128], first], axis=0
        )
        pair_gram += exact_across(pair, tall(pair))
    gram_ref[...] = beside(
        pair_gram[:size], pltpu.roll(window(pair_gram[size:], 1), size, 1)
    )


def tall(flat):
    rest = flat.shape[1] - flat.shape[0]
    return jnp.concatenate([flat, jnp.zeros((rest, flat.shape[1]), flat.dtype)], axis=0)


def flipped(flat):
    return tall(flat).T[: flat.shape[0]]


def times(left, right):
    return exact_plain(left, tall(right))


def beside(left, right):
    return left + pltpu.roll(right, left.shape[0], 1)


def stacked(upper, lower):
    rest = jnp.zeros((upper.shape[1] - 2 * upper.shape[0], upper.shape[1]), upper.dtype)
    return jnp.concatenate([upper, lower, rest], axis=0)


def sandwich(rows, middle):
    return exact_across(exact_plain(rows, middle), tall(rows))


def symmetric(flat):
    return 0.5 * (flat + flipped(flat))


def window(flat, place):
    size = flat.shape[0]
    if place:
        flat = pltpu.roll(flat, flat.shape[1] - place * size, 1)
    lanes = lax.broadcasted_iota(jnp.int32, flat.shape, 1)
    return jnp.where(lanes < size, flat, 0.0)


def solve_many(pairs):
    size = pairs[0][0].shape[0]
    systems = [matrix + pltpu.roll(side, size, 1) for matrix, side in pairs]
    sublanes = lax.broadcasted_iota(jnp.int32, systems[0].shape, 0)
    for pivot in range(size):
        updated = []
        for system in systems:
            column = system[:, pivot : pivot + 1]
            row = system[pivot : pivot + 1, :] / column[pivot : pivot + 1, :]
            updated.append(jnp.where(sublanes == pivot, row, system - column * row))
        systems = updated
    return [window(system, 1) for system in systems]


def close_kernel(piece_count, *refs):
    part_refs = refs[:piece_count]
    *gram_refs, scaling_ref, query_ref, first_ref, solution_ref, residual_ref = refs[piece_count:]
    size = query_ref.shape[0]
    weight = graph_weight
    total = total_of(gram_refs)
    g00 = symmetric(window(total, 0))
    g01 = window(total, 1)
    g11 = symmetric(window(total, 2))
    g12 = symmetric(window(total, 3))
    eye = (
        lax.broadcasted_iota(jnp.int32, total.shape, 0)
        == lax.broadcasted_iota(jnp.int32, total.shape, 1)
    ).astype(jnp.float32)
    curve = symmetric(g00 - weight * g01)
    steps, inverse = solve_many([(curve, g00), (g00, eye)])
    steps_t = flipped(steps)
    plain_gram = stacked(beside(g00, g01), beside(flipped(g01), g11))
    through_gram = stacked(beside(g01, g11), beside(g11, g12))
    after_first = beside(eye - steps_t, weight * steps_t)
    new_gram = symmetric(sandwich(after_first, plain_gram))
    mixing = times(inverse, new_gram)
    direction = after_first + flipped(mixing)
    curve = symmetric(sandwich(direction, plain_gram - weight * through_gram))
    (steps,) = solve_many([(curve, new_gram)])
    steps_t2 = flipped(steps)
    applied = direction - weight * pltpu.roll(direction, size, 1)
    solution_rows = exact_plain(beside(eye, steps_t2), stacked(steps_t, direction))
    residual_rows = exact_plain(beside(eye, -steps_t2), stacked(after_first, applied))
    rows = jnp.concatenate([solution_rows, residual_rows], axis=0)
    for part in range(first_ref.shape[0]):
        lanes = slice(part * 128, part * 128 + 128)
        basis = jnp.concatenate(
            [
                query_ref[:, lanes],
                first_ref[part],
                scaled_sum(part_refs, scaling_ref, part),
                jnp.zeros_like(eye),
            ],
            axis=0,
        )
        values = exact_plain(rows, basis)
        solution_ref[:, lanes] = values[:size]
        residual_ref[:, lanes] = values[size:]


def pass_around(pieces, axis):
    count = len(pieces)
    return [pieces[0]] + [
        lax.ppermute(pieces[ahead], axis, [(at, (at + ahead) % count) for at in range(count)])
        for ahead in range(1, count)
    ]


def spread(piece, axis):
    return pass_around([piece] * lax.axis_size(axis), axis)


def simple_call(kernel, shapes, name, *operands):
    return pl.pallas_call(
        kernel,
        out_shape=shapes,
        compiler_params=pltpu.CompilerParams(vmem_limit_bytes=VMEM_LIMIT),
        name=name,
    )(*operands)


def sum_kernel(*refs):
    refs[-1][...] = total_of(refs[:-1])


def body(queries, block_spots, live_blocks, neighbor_cols, neighbor_sims):
    row_count = lax.axis_size("row")
    col_count = lax.axis_size("col")
    query_rows, seg_len = queries.shape
    per_seg = seg_len // 128
    spots = block_spots[0, 0]
    facts = jnp.stack([live_blocks[0, 0], lax.axis_index("row"), lax.axis_index("col")])
    piece = (per_seg, query_rows, 128)
    wide = jax.ShapeDtypeStruct(piece, jnp.float32)
    narrow = jax.ShapeDtypeStruct(piece, jnp.bfloat16)
    gram_shape = jax.ShapeDtypeStruct((query_rows, 128), jnp.float32)

    blocks, *sums = build_blocks(
        spots, facts, neighbor_cols[0, 0], neighbor_sims[0, 0], row_count, col_count, per_seg
    )
    row_parts = pass_around(sums[:row_count], "row")
    col_parts = pass_around(sums[row_count:], "col")
    scaling, scaled = simple_call(
        start_kernel,
        [jax.ShapeDtypeStruct((per_seg, 128), jnp.float32), narrow],
        "start",
        *row_parts,
        *col_parts,
        queries,
    )

    def product(vectors, gram=None):
        totals = block_products(
            spots, facts, blocks, spread(vectors, "row"), spread(vectors, "col"), gram
        )
        devices = row_count + col_count
        parts = pass_around(totals[:row_count], "row")
        parts += pass_around(totals[row_count:devices], "col")
        return parts, totals[devices:]

    parts, _ = product(scaled)
    first, scaled, gram = simple_call(
        middle_kernel, [wide, narrow, gram_shape], "middle", *parts, scaling, queries
    )
    parts, (gram,) = product(scaled, gram)
    (gram,) = simple_call(sum_kernel, [gram_shape], "gram_sum", *spread(gram, "row"))
    flat = jax.ShapeDtypeStruct(queries.shape, jnp.float32)
    return tuple(
        simple_call(
            functools.partial(close_kernel, len(parts)),
            [flat, flat],
            "close",
            *parts,
            *spread(gram, "col"),
            scaling,
            queries,
            first,
        )
    )


def solution(mesh):
    placed = (
        P(None, ("row", "col")),
        P("row", "col", None),
        P("row", "col"),
        P("row", "col", None, None, None),
        P("row", "col", None, None, None),
    )
    return jax.shard_map(
        body,
        mesh=mesh,
        in_specs=placed,
        out_specs=(P(None, ("row", "col")), P(None, ("row", "col"))),
        check_vma=False,
    )
```

time: 175 us -> 168 us (0.960); the launches traced: 175 us -> 165 us
  blocking collectives: 131 us -> 0 us
  starting transfers between devices: 7.59 us -> 82.8 us
  waiting for transfers between devices: 3.8 us -> 30 us
  Pallas kernels: 25.5 us -> 46.1 us
  local copies, waits for them, and re-layouts: 5.84 us -> 4.01 us
    all_to_all x10 -> x0, blocking collectives: 131 us -> none  [exchange(): return lax.all_to_all(parts, axis, 0, 0, tiled=True)]
    ppermute x0 -> x60, starting transfers between devices: none -> 82.8 us  [pass_around(): lax.ppermute(pieces[ahead], axis, [(at, (at + ahead) % count) for at in r...]
    ppermute x0 -> x60, waiting for transfers between devices: none -> 30 us  [pass_around(): lax.ppermute(pieces[ahead], axis, [(at, (at + ahead) % count) for at in r...]
    pallas_call x3, Pallas kernels: 16.4 us -> 31.4 us  [the longest x2 19.7 us: block_products(): pl.pallas_call(functools.partial(product_kernel, len(row_pieces), len(col...]
    all_to_all x1 -> x0, starting transfers between devices: 7.59 us -> none  [exchange(): return lax.all_to_all(parts, axis, 0, 0, tiled=True)]
    pallas_call x4, Pallas kernels: 9.06 us -> 14.7 us  [simple_call(): pl.pallas_call(kernel, out_shape=shapes, compiler_params=pltpu.CompilerPa...]
    all_to_all x1 -> x0, waiting for transfers between devices: 3.8 us -> none  [exchange(): return lax.all_to_all(parts, axis, 0, 0, tiled=True)]
    unnamed x14 -> x120, local copies, waits for them, and re-layouts: 5.02 us -> 4.01 us
  transfers between devices with their start and end apart: 1 -> 60, of which waited for: 1 -> 27; matrix products, arithmetic and copies ran while one was open for 0% -> 0% of each run, Pallas kernels for 0% -> 0%
where the time goes in v2:
time: 168 us; the launch traced here: 165 us
  starting transfers between devices  82.8 us (49%)
  Pallas kernels  46.1 us (27%)
  waiting for transfers between devices  30 us (18%)
  local copies, waits for them, and re-layouts  4.01 us (2%)
  between operations  1.89 us (1%)
    ppermute x60, starting transfers between devices, pass_around(): lax.ppermute(pieces[ahead], axis, [(at, (at + ahead) % count) for at in r...  82.8 us
    ppermute x60, waiting for transfers between devices, pass_around(): lax.ppermute(pieces[ahead], axis, [(at, (at + ahead) % count) for at in r...  30 us
    pallas_call x2, Pallas kernels, block_products(): pl.pallas_call(functools.partial(product_kernel, len(row_pieces), len(col...  19.7 us
    pallas_call x4, Pallas kernels, simple_call(): pl.pallas_call(kernel, out_shape=shapes, compiler_params=pltpu.CompilerPa...  14.7 us
    pallas_call x1, Pallas kernels, build_blocks(): pl.pallas_call(functools.partial(build_kernel, row_count, col_count, per_...  11.7 us
    unnamed x120, local copies, waits for them, and re-layouts  4.01 us
  transfers between devices with their start and end apart: 60, of which 27 were waited for; matrix products, arithmetic and copies ran while one was open for 0% of the time, Pallas kernels for 0%

profile of v2, /device:TPU:0, one launch (start us, length us, event | category | flops | bytes accessed | tf_op | source)
XLA Modules:
  0.0 165.4 jit_solution(2753528463050648283)
XLA Ops:
  1.9 11.7 %build_blocks.1 = (bf16[256,128,128]{2,1,0:T(8,128)(2,1)}, f32[4,128]{1,0:T(4,128)}, f32[4,128]{1,0:T(4,128)}, f32[4,128]{1,0:T(4,128)}, f32[4,128]{1,0:T(4,128)...) custom-call(s32[256]{0:T(256)} %bitcast.9, ...), custom_call_target="tpu_custom_call" | custom-call | tf_op jit(solution)/shard_map/build_blocks/pallas_call | solution.py:103
  13.6 1.6 collective-permute-start
  15.2 11.1 %collective-permute-start.1 = (f32[4,128]{1,0:T(4,128)}, f32[4,128]{1,0:T(4,128)S(1)}, u32[]{:S(2)}, u32[]{:S(2)}) collective-permute-start(f32[4,128]{1,0:T(4,128)} %get-tuple-element.48), channel_id=1, source_target_pairs={{0,16},{8,24},{16,0},{24,8},{1,17},{9,25},{17,1},{25,9},{2,18},{10... | collective-permute-start | bytes 6152 | tf_op jit(solution)/shard_map/ppermute | solution.py:375
  28.1 3.6 %collective-permute-start.6 = (f32[4,128]{1,0:T(4,128)}, f32[4,128]{1,0:T(4,128)S(1)}, u32[]{:S(2)}, u32[]{:S(2)}) collective-permute-start(f32[4,128]{1,0:T(4,128)} %get-tuple-element.54), channel_id=1, source_target_pairs={{0,4},{1,5},{2,6},{3,7},{4,0},{5,1},{6,2},{7,3},{8,12},{9,13},{10,... | collective-permute-start | bytes 6152 | tf_op jit(solution)/shard_map/ppermute | solution.py:375
  32.8 1.8 %collective-permute-start.8 = (f32[4,128]{1,0:T(4,128)}, f32[4,128]{1,0:T(4,128)S(1)}, u32[]{:S(2)}, u32[]{:S(2)}) collective-permute-start(f32[4,128]{1,0:T(4,128)} %get-tuple-element.56), channel_id=1, source_target_pairs={{0,6},{1,7},{2,0},{3,1},{4,2},{5,3},{6,4},{7,5},{8,14},{9,15},{10,... | collective-permute-start | bytes 6152 | tf_op jit(solution)/shard_map/ppermute | solution.py:375
  36.6 1.8 %collective-permute-done.9.refs_11_ = f32[4,128]{1,0:T(4,128)S(1)} collective-permute-done((f32[4,128]{1,0:T(4,128)}, f32[4,128]{1,0:T(4,128)S(1)}, u32[]{:S(2)}, u32[]{:S(2)}) %collective-permute-start.9) | collective-permute-done | bytes 2080 | tf_op jit(solution)/shard_map/ppermute | solution.py:375
  40.6 4.2 %collective-permute-start.19 = (bf16[4,32,128]{2,1,0:T(8,128)(2,1)}, bf16[4,32,128]{2,1,0:T(8,128)(2,1)S(1)}, u32[]{:S(2)}, u32[]{:S(2)}) collective-permute-start(bf16[4,32,128]{2,1,0:T(8,128)(2,1)} %get-tuple-element.58.refs_0_.refs_4_), channel_id=1, source_target_pairs={{0,7},{1,0},{2,1},{3,2},{4,3},{5,4},{6,5},{7,6},{8,15},{9,8},{10,9... | collective-permute-start | bytes 98312 | tf_op jit(solution)/shard_map/ppermute | solution.py:375
  45.9 1.9 %collective-permute-start.16 = (bf16[4,32,128]{2,1,0:T(8,128)(2,1)}, bf16[4,32,128]{2,1,0:T(8,128)(2,1)S(1)}, u32[]{:S(2)}, u32[]{:S(2)}) collective-permute-start(bf16[4,32,128]{2,1,0:T(8,128)(2,1)} %get-tuple-element.58.refs_0_.refs_4_), channel_id=1, source_target_pairs={{0,4},{1,5},{2,6},{3,7},{4,0},{5,1},{6,2},{7,3},{8,12},{9,13},{10,... | collective-permute-start | bytes 98312 | tf_op jit(solution)/shard_map/ppermute | solution.py:375
  48.8 2.9 %collective-permute-start.14 = (bf16[4,32,128]{2,1,0:T(8,128)(2,1)}, bf16[4,32,128]{2,1,0:T(8,128)(2,1)S(1)}, u32[]{:S(2)}, u32[]{:S(2)}) collective-permute-start(bf16[4,32,128]{2,1,0:T(8,128)(2,1)} %get-tuple-element.58.refs_0_.refs_4_), channel_id=1, source_target_pairs={{0,2},{1,3},{2,4},{3,5},{4,6},{5,7},{6,0},{7,1},{8,10},{9,11},{10,... | collective-permute-start | bytes 98312 | tf_op jit(solution)/shard_map/ppermute | solution.py:375
  55.4 3.1 %collective-permute-done.13.refs_5_ = bf16[4,32,128]{2,1,0:T(8,128)(2,1)S(1)} collective-permute-done((bf16[4,32,128]{2,1,0:T(8,128)(2,1)}, bf16[4,32,128]{2,1,0:T(8,128)(2,1)S(1)}, u32[]{:S(2)}, u32[]{:S(2)}) %collective-permute-start.13) | collective-permute-done | bytes 32800 | tf_op jit(solution)/shard_map/ppermute | solution.py:375
  59.2 9.2 %block_products.2 = (bf16[4,32,128]{2,1,0:T(8,128)(2,1)}, bf16[4,32,128]{2,1,0:T(8,128)(2,1)}, bf16[4,32,128]{2,1,0:T(8,128)(2,1)}, bf16[4,32,128]{2,1,0:T(8,128...) custom-call(s32[256]{0:T(256)} %bitcast.10, ...), custom_call_target="tpu_custom_call" | custom-call | tf_op jit(solution)/shard_map/block_products/pallas_call | solution.py:213
  68.4 5.7 %collective-permute-start.21 = (bf16[4,32,128]{2,1,0:T(8,128)(2,1)}, bf16[4,32,128]{2,1,0:T(8,128)(2,1)S(1)}, u32[]{:S(2)}, u32[]{:S(2)}) collective-permute-start(bf16[4,32,128]{2,1,0:T(8,128)(2,1)} %get-tuple-element.61), channel_id=1, source_target_pairs={{0,16},{8,24},{16,0},{24,8},{1,17},{9,25},{17,1},{25,9},{2,18},{10... | collective-permute-start | bytes 98312 | tf_op jit(solution)/shard_map/ppermute | solution.py:375
  76.2 3.2 %collective-permute-start.26 = (bf16[4,32,128]{2,1,0:T(8,128)(2,1)}, bf16[4,32,128]{2,1,0:T(8,128)(2,1)S(1)}, u32[]{:S(2)}, u32[]{:S(2)}) collective-permute-start(bf16[4,32,128]{2,1,0:T(8,128)(2,1)} %get-tuple-element.67), channel_id=1, source_target_pairs={{0,4},{1,5},{2,6},{3,7},{4,0},{5,1},{6,2},{7,3},{8,12},{9,13},{10,... | collective-permute-start | bytes 98312 | tf_op jit(solution)/shard_map/ppermute | solution.py:375
  79.6 1.7 %collective-permute-done.23.refs_5_ = bf16[4,32,128]{2,1,0:T(8,128)(2,1)S(1)} collective-permute-done((bf16[4,32,128]{2,1,0:T(8,128)(2,1)}, bf16[4,32,128]{2,1,0:T(8,128)(2,1)S(1)}, u32[]{:S(2)}, u32[]{:S(2)}) %collective-permute-start.23) | collective-permute-done | bytes 32800 | tf_op jit(solution)/shard_map/ppermute | solution.py:375
  82.4 1.9 %collective-permute-start.29 = (bf16[4,32,128]{2,1,0:T(8,128)(2,1)}, bf16[4,32,128]{2,1,0:T(8,128)(2,1)S(1)}, u32[]{:S(2)}, u32[]{:S(2)}) collective-permute-start(bf16[4,32,128]{2,1,0:T(8,128)(2,1)} %get-tuple-element.70), channel_id=1, source_target_pairs={{0,7},{1,0},{2,1},{3,2},{4,3},{5,4},{6,5},{7,6},{8,15},{9,8},{10,9... | collective-permute-start | bytes 98312 | tf_op jit(solution)/shard_map/ppermute | solution.py:375
  87.1 2.2 %middle.1 = (f32[4,32,128]{2,1,0:T(8,128)}, bf16[4,32,128]{2,1,0:T(8,128)(2,1)}, f32[32,128]{1,0:T(8,128)}) custom-call(bf16[4,32,128]{2,1,0:T(8,128)(2,1)} %get-tuple-element.59.refs_0_, bf16[4,32,128]{2,1,0:T(8,128)(2,1)} %copy-done.20, bf16[4,32,128]{2,1,0:T(8,128)(2,1)} %copy-done.21, bf16[4,32,128]{2,1,0:T(8,128)(2,1)} %copy-done.22, ...), custom_call_target="tpu_custom_call" | custom-call | tf_op jit(solution)/shard_map/middle/pallas_call | solution.py:385
  89.3 4.6 %collective-permute-start.39 = (bf16[4,32,128]{2,1,0:T(8,128)(2,1)}, bf16[4,32,128]{2,1,0:T(8,128)(2,1)S(1)}, u32[]{:S(2)}, u32[]{:S(2)}) collective-permute-start(bf16[4,32,128]{2,1,0:T(8,128)(2,1)} %get-tuple-element.72.refs_0_.refs_4_), channel_id=1, source_target_pairs={{0,7},{1,0},{2,1},{3,2},{4,3},{5,4},{6,5},{7,6},{8,15},{9,8},{10,9... | collective-permute-start | bytes 98312 | tf_op jit(solution)/shard_map/ppermute | solution.py:375
  94.6 2.3 %collective-permute-start.36 = (bf16[4,32,128]{2,1,0:T(8,128)(2,1)}, bf16[4,32,128]{2,1,0:T(8,128)(2,1)S(1)}, u32[]{:S(2)}, u32[]{:S(2)}) collective-permute-start(bf16[4,32,128]{2,1,0:T(8,128)(2,1)} %get-tuple-element.72.refs_0_.refs_4_), channel_id=1, source_target_pairs={{0,4},{1,5},{2,6},{3,7},{4,0},{5,1},{6,2},{7,3},{8,12},{9,13},{10,... | collective-permute-start | bytes 98312 | tf_op jit(solution)/shard_map/ppermute | solution.py:375
  97.6 2.9 %collective-permute-start.34 = (bf16[4,32,128]{2,1,0:T(8,128)(2,1)}, bf16[4,32,128]{2,1,0:T(8,128)(2,1)S(1)}, u32[]{:S(2)}, u32[]{:S(2)}) collective-permute-start(bf16[4,32,128]{2,1,0:T(8,128)(2,1)} %get-tuple-element.72.refs_0_.refs_4_), channel_id=1, source_target_pairs={{0,2},{1,3},{2,4},{3,5},{4,6},{5,7},{6,0},{7,1},{8,10},{9,11},{10,... | collective-permute-start | bytes 98312 | tf_op jit(solution)/shard_map/ppermute | solution.py:375
  103.0 1.6 collective-permute-done.34.refs_6_
  104.6 2.7 %collective-permute-done.33.refs_5_ = bf16[4,32,128]{2,1,0:T(8,128)(2,1)S(1)} collective-permute-done((bf16[4,32,128]{2,1,0:T(8,128)(2,1)}, bf16[4,32,128]{2,1,0:T(8,128)(2,1)S(1)}, u32[]{:S(2)}, u32[]{:S(2)}) %collective-permute-start.33) | collective-permute-done | bytes 32800 | tf_op jit(solution)/shard_map/ppermute | solution.py:375
  107.9 10.5 %block_products.3 = (bf16[4,32,128]{2,1,0:T(8,128)(2,1)}, bf16[4,32,128]{2,1,0:T(8,128)(2,1)}, bf16[4,32,128]{2,1,0:T(8,128)(2,1)}, bf16[4,32,128]{2,1,0:T(8,128...) custom-call(s32[256]{0:T(256)} %bitcast.11, ...), custom_call_target="tpu_custom_call" | custom-call | tf_op jit(solution)/shard_map/block_products/pallas_call | solution.py:213
  118.4 5.3 %collective-permute-start.52 = (f32[32,128]{1,0:T(8,128)}, f32[32,128]{1,0:T(8,128)S(1)}, u32[]{:S(2)}, u32[]{:S(2)}) collective-permute-start(f32[32,128]{1,0:T(8,128)} %get-tuple-element.86.refs_0_), channel_id=1, source_target_pairs={{0,24},{8,0},{16,8},{24,16},{1,25},{9,1},{17,9},{25,17},{2,26},{10... | collective-permute-start | bytes 49160 | tf_op jit(solution)/shard_map/ppermute | solution.py:375
  125.4 2.3 %collective-permute-done.51.refs_2_ = f32[32,128]{1,0:T(8,128)S(1)} collective-permute-done((f32[32,128]{1,0:T(8,128)}, f32[32,128]{1,0:T(8,128)S(1)}, u32[]{:S(2)}, u32[]{:S(2)}) %collective-permute-start.51) | collective-permute-done | bytes 16416 | tf_op jit(solution)/shard_map/ppermute | solution.py:375
  130.3 4.3 %collective-permute-start.56 = (f32[32,128]{1,0:T(8,128)}, f32[32,128]{1,0:T(8,128)S(1)}, u32[]{:S(2)}, u32[]{:S(2)}) collective-permute-start(f32[32,128]{1,0:T(8,128)} %gram_sum.1.refs_12_), channel_id=1, source_target_pairs={{0,4},{1,5},{2,6},{3,7},{4,0},{5,1},{6,2},{7,3},{8,12},{9,13},{10,... | collective-permute-start | bytes 49160 | tf_op jit(solution)/shard_map/ppermute | solution.py:375
  134.7 2.1 %collective-permute-start.54 = (f32[32,128]{1,0:T(8,128)}, f32[32,128]{1,0:T(8,128)S(1)}, u32[]{:S(2)}, u32[]{:S(2)}) collective-permute-start(f32[32,128]{1,0:T(8,128)} %gram_sum.1.refs_12_), channel_id=1, source_target_pairs={{0,2},{1,3},{2,4},{3,5},{4,6},{5,7},{6,0},{7,1},{8,10},{9,11},{10,... | collective-permute-start | bytes 49160 | tf_op jit(solution)/shard_map/ppermute | solution.py:375
  140.6 2.0 %collective-permute-start.43 = (bf16[4,32,128]{2,1,0:T(8,128)(2,1)}, bf16[4,32,128]{2,1,0:T(8,128)(2,1)S(1)}, u32[]{:S(2)}, u32[]{:S(2)}) collective-permute-start(bf16[4,32,128]{2,1,0:T(8,128)(2,1)} %get-tuple-element.79), channel_id=1, source_target_pairs={{0,1},{1,2},{2,3},{3,4},{4,5},{5,6},{6,7},{7,0},{8,9},{9,10},{10,1... | collective-permute-start | bytes 98312 | tf_op jit(solution)/shard_map/ppermute | solution.py:375
  143.4 1.6 collective-permute-start.45
  145.0 2.8 %collective-permute-start.46 = (bf16[4,32,128]{2,1,0:T(8,128)(2,1)}, bf16[4,32,128]{2,1,0:T(8,128)(2,1)S(1)}, u32[]{:S(2)}, u32[]{:S(2)}) collective-permute-start(bf16[4,32,128]{2,1,0:T(8,128)(2,1)} %get-tuple-element.82), channel_id=1, source_target_pairs={{0,4},{1,5},{2,6},{3,7},{4,0},{5,1},{6,2},{7,3},{8,12},{9,13},{10,... | collective-permute-start | bytes 98312 | tf_op jit(solution)/shard_map/ppermute | solution.py:375
  148.9 2.3 %collective-permute-start.48 = (bf16[4,32,128]{2,1,0:T(8,128)(2,1)}, bf16[4,32,128]{2,1,0:T(8,128)(2,1)S(1)}, u32[]{:S(2)}, u32[]{:S(2)}) collective-permute-start(bf16[4,32,128]{2,1,0:T(8,128)(2,1)} %get-tuple-element.84), channel_id=1, source_target_pairs={{0,6},{1,7},{2,0},{3,1},{4,2},{5,3},{6,4},{7,5},{8,14},{9,15},{10,... | collective-permute-start | bytes 98312 | tf_op jit(solution)/shard_map/ppermute | solution.py:375
  151.2 2.0 %collective-permute-start.49 = (bf16[4,32,128]{2,1,0:T(8,128)(2,1)}, bf16[4,32,128]{2,1,0:T(8,128)(2,1)S(1)}, u32[]{:S(2)}, u32[]{:S(2)}) collective-permute-start(bf16[4,32,128]{2,1,0:T(8,128)(2,1)} %get-tuple-element.85), channel_id=1, source_target_pairs={{0,7},{1,0},{2,1},{3,2},{4,3},{5,4},{6,5},{7,6},{8,15},{9,8},{10,9... | collective-permute-start | bytes 98312 | tf_op jit(solution)/shard_map/ppermute | solution.py:375
  155.9 9.6 %close.1 = (f32[32,512]{1,0:T(8,128)}, f32[32,512]{1,0:T(8,128)}) custom-call(bf16[4,32,128]{2,1,0:T(8,128)(2,1)} %get-tuple-element.74.refs_0_, bf16[4,32,128]{2,1,0:T(8,128)(2,1)} %copy-done.30, bf16[4,32,128]{2,1,0:T(8,128)(2,1)} %copy-done.31, bf16[4,32,128]{2,1,0:T(8,128)(2,1)} %copy-done.32, bf16[4,32,128]{2,1,0:T(8,128)(2,1)} %get-tuple-element.78.refs_4_, ...), custom_call_target="tpu_custom_call" | custom-call | tf_op jit(solution)/shard_map/close/pallas_call | solution.py:385
  (216 shorter events, 37.4 us)
Async XLA Ops:
  13.6 13.8 %collective-permute-start = (f32[4,128]{1,0:T(4,128)}, f32[4,128]{1,0:T(4,128)S(1)}, u32[]{:S(2)}, u32[]{:S(2)}) collective-permute-start(f32[4,128]{1,0:T(4,128)} %get-tuple-element.47), channel_id=1, source_target_pairs={{0,8},{8,16},{16,24},{24,0},{1,9},{9,17},{17,25},{25,1},{2,10},{10... | collective-permute-start | bytes 6152 | tf_op jit(solution)/shard_map/ppermute | solution.py:375
  15.2 12.9 %collective-permute-start.1 = (f32[4,128]{1,0:T(4,128)}, f32[4,128]{1,0:T(4,128)S(1)}, u32[]{:S(2)}, u32[]{:S(2)}) collective-permute-start(f32[4,128]{1,0:T(4,128)} %get-tuple-element.48), channel_id=1, source_target_pairs={{0,16},{8,24},{16,0},{24,8},{1,17},{9,25},{17,1},{25,9},{2,18},{10... | collective-permute-start | bytes 6152 | tf_op jit(solution)/shard_map/ppermute | solution.py:375
  26.4 8.3 %collective-permute-start.4 = (f32[4,128]{1,0:T(4,128)}, f32[4,128]{1,0:T(4,128)S(1)}, u32[]{:S(2)}, u32[]{:S(2)}) collective-permute-start(f32[4,128]{1,0:T(4,128)} %get-tuple-element.52), channel_id=1, source_target_pairs={{0,2},{1,3},{2,4},{3,5},{4,6},{5,7},{6,0},{7,1},{8,10},{9,11},{10,... | collective-permute-start | bytes 6152 | tf_op jit(solution)/shard_map/ppermute | solution.py:375
  27.4 8.7 %collective-permute-start.5 = (f32[4,128]{1,0:T(4,128)}, f32[4,128]{1,0:T(4,128)S(1)}, u32[]{:S(2)}, u32[]{:S(2)}) collective-permute-start(f32[4,128]{1,0:T(4,128)} %get-tuple-element.53), channel_id=1, source_target_pairs={{0,3},{1,4},{2,5},{3,6},{4,7},{5,0},{6,1},{7,2},{8,11},{9,12},{10,... | collective-permute-start | bytes 6152 | tf_op jit(solution)/shard_map/ppermute | solution.py:375
  28.1 8.0 %collective-permute-start.6 = (f32[4,128]{1,0:T(4,128)}, f32[4,128]{1,0:T(4,128)S(1)}, u32[]{:S(2)}, u32[]{:S(2)}) collective-permute-start(f32[4,128]{1,0:T(4,128)} %get-tuple-element.54), channel_id=1, source_target_pairs={{0,4},{1,5},{2,6},{3,7},{4,0},{5,1},{6,2},{7,3},{8,12},{9,13},{10,... | collective-permute-start | bytes 6152 | tf_op jit(solution)/shard_map/ppermute | solution.py:375
  40.6 8.2 %collective-permute-start.19 = (bf16[4,32,128]{2,1,0:T(8,128)(2,1)}, bf16[4,32,128]{2,1,0:T(8,128)(2,1)S(1)}, u32[]{:S(2)}, u32[]{:S(2)}) collective-permute-start(bf16[4,32,128]{2,1,0:T(8,128)(2,1)} %get-tuple-element.58.refs_0_.refs_4_), channel_id=1, source_target_pairs={{0,7},{1,0},{2,1},{3,2},{4,3},{5,4},{6,5},{7,6},{8,15},{9,8},{10,9... | collective-permute-start | bytes 98312 | tf_op jit(solution)/shard_map/ppermute | solution.py:375
  44.8 6.9 %collective-permute-start.18 = (bf16[4,32,128]{2,1,0:T(8,128)(2,1)}, bf16[4,32,128]{2,1,0:T(8,128)(2,1)S(1)}, u32[]{:S(2)}, u32[]{:S(2)}) collective-permute-start(bf16[4,32,128]{2,1,0:T(8,128)(2,1)} %get-tuple-element.58.refs_0_.refs_4_), channel_id=1, source_target_pairs={{0,6},{1,7},{2,0},{3,1},{4,2},{5,3},{6,4},{7,5},{8,14},{9,15},{10,... | collective-permute-start | bytes 98312 | tf_op jit(solution)/shard_map/ppermute | solution.py:375
  44.8 6.9 %collective-permute-start.17 = (bf16[4,32,128]{2,1,0:T(8,128)(2,1)}, bf16[4,32,128]{2,1,0:T(8,128)(2,1)S(1)}, u32[]{:S(2)}, u32[]{:S(2)}) collective-permute-start(bf16[4,32,128]{2,1,0:T(8,128)(2,1)} %get-tuple-element.58.refs_0_.refs_4_), channel_id=1, source_target_pairs={{0,5},{1,6},{2,7},{3,0},{4,1},{5,2},{6,3},{7,4},{8,13},{9,14},{10,... | collective-permute-start | bytes 98312 | tf_op jit(solution)/shard_map/ppermute | solution.py:375
  48.8 6.6 %collective-permute-start.14 = (bf16[4,32,128]{2,1,0:T(8,128)(2,1)}, bf16[4,32,128]{2,1,0:T(8,128)(2,1)S(1)}, u32[]{:S(2)}, u32[]{:S(2)}) collective-permute-start(bf16[4,32,128]{2,1,0:T(8,128)(2,1)} %get-tuple-element.58.refs_0_.refs_4_), channel_id=1, source_target_pairs={{0,2},{1,3},{2,4},{3,5},{4,6},{5,7},{6,0},{7,1},{8,10},{9,11},{10,... | collective-permute-start | bytes 98312 | tf_op jit(solution)/shard_map/ppermute | solution.py:375
  51.7 6.8 %collective-permute-start.13 = (bf16[4,32,128]{2,1,0:T(8,128)(2,1)}, bf16[4,32,128]{2,1,0:T(8,128)(2,1)S(1)}, u32[]{:S(2)}, u32[]{:S(2)}) collective-permute-start(bf16[4,32,128]{2,1,0:T(8,128)(2,1)} %get-tuple-element.58.refs_0_.refs_4_), channel_id=1, source_target_pairs={{0,1},{1,2},{2,3},{3,4},{4,5},{5,6},{6,7},{7,0},{8,9},{9,10},{10,1... | collective-permute-start | bytes 98312 | tf_op jit(solution)/shard_map/ppermute | solution.py:375
  51.7 6.8 %collective-permute-start.12 = (bf16[4,32,128]{2,1,0:T(8,128)(2,1)}, bf16[4,32,128]{2,1,0:T(8,128)(2,1)S(1)}, u32[]{:S(2)}, u32[]{:S(2)}) collective-permute-start(bf16[4,32,128]{2,1,0:T(8,128)(2,1)} %get-tuple-element.58.refs_0_.refs_4_), channel_id=1, source_target_pairs={{0,24},{8,0},{16,8},{24,16},{1,25},{9,1},{17,9},{25,17},{2,26},{10... | collective-permute-start | bytes 98312 | tf_op jit(solution)/shard_map/ppermute | solution.py:375
  51.9 6.6 %collective-permute-start.11 = (bf16[4,32,128]{2,1,0:T(8,128)(2,1)}, bf16[4,32,128]{2,1,0:T(8,128)(2,1)S(1)}, u32[]{:S(2)}, u32[]{:S(2)}) collective-permute-start(bf16[4,32,128]{2,1,0:T(8,128)(2,1)} %get-tuple-element.58.refs_0_.refs_4_), channel_id=1, source_target_pairs={{0,16},{8,24},{16,0},{24,8},{1,17},{9,25},{17,1},{25,9},{2,18},{10... | collective-permute-start | bytes 98312 | tf_op jit(solution)/shard_map/ppermute | solution.py:375
  68.3 7.1 %collective-permute-start.20 = (bf16[4,32,128]{2,1,0:T(8,128)(2,1)}, bf16[4,32,128]{2,1,0:T(8,128)(2,1)S(1)}, u32[]{:S(2)}, u32[]{:S(2)}) collective-permute-start(bf16[4,32,128]{2,1,0:T(8,128)(2,1)} %get-tuple-element.60), channel_id=1, source_target_pairs={{0,8},{8,16},{16,24},{24,0},{1,9},{9,17},{17,25},{25,1},{2,10},{10... | collective-permute-start | bytes 98312 | tf_op jit(solution)/shard_map/ppermute | solution.py:375
  68.4 7.8 %collective-permute-start.21 = (bf16[4,32,128]{2,1,0:T(8,128)(2,1)}, bf16[4,32,128]{2,1,0:T(8,128)(2,1)S(1)}, u32[]{:S(2)}, u32[]{:S(2)}) collective-permute-start(bf16[4,32,128]{2,1,0:T(8,128)(2,1)} %get-tuple-element.61), channel_id=1, source_target_pairs={{0,16},{8,24},{16,0},{24,8},{1,17},{9,25},{17,1},{25,9},{2,18},{10... | collective-permute-start | bytes 98312 | tf_op jit(solution)/shard_map/ppermute | solution.py:375
  74.1 7.2 %collective-permute-start.23 = (bf16[4,32,128]{2,1,0:T(8,128)(2,1)}, bf16[4,32,128]{2,1,0:T(8,128)(2,1)S(1)}, u32[]{:S(2)}, u32[]{:S(2)}) collective-permute-start(bf16[4,32,128]{2,1,0:T(8,128)(2,1)} %get-tuple-element.64), channel_id=1, source_target_pairs={{0,1},{1,2},{2,3},{3,4},{4,5},{5,6},{6,7},{7,0},{8,9},{9,10},{10,1... | collective-permute-start | bytes 98312 | tf_op jit(solution)/shard_map/ppermute | solution.py:375
  74.1 8.3 %collective-permute-start.24 = (bf16[4,32,128]{2,1,0:T(8,128)(2,1)}, bf16[4,32,128]{2,1,0:T(8,128)(2,1)S(1)}, u32[]{:S(2)}, u32[]{:S(2)}) collective-permute-start(bf16[4,32,128]{2,1,0:T(8,128)(2,1)} %get-tuple-element.65), channel_id=1, source_target_pairs={{0,2},{1,3},{2,4},{3,5},{4,6},{5,7},{6,0},{7,1},{8,10},{9,11},{10,... | collective-permute-start | bytes 98312 | tf_op jit(solution)/shard_map/ppermute | solution.py:375
  75.5 8.8 %collective-permute-start.25 = (bf16[4,32,128]{2,1,0:T(8,128)(2,1)}, bf16[4,32,128]{2,1,0:T(8,128)(2,1)S(1)}, u32[]{:S(2)}, u32[]{:S(2)}) collective-permute-start(bf16[4,32,128]{2,1,0:T(8,128)(2,1)} %get-tuple-element.66), channel_id=1, source_target_pairs={{0,3},{1,4},{2,5},{3,6},{4,7},{5,0},{6,1},{7,2},{8,11},{9,12},{10,... | collective-permute-start | bytes 98312 | tf_op jit(solution)/shard_map/ppermute | solution.py:375
  76.2 8.1 %collective-permute-start.26 = (bf16[4,32,128]{2,1,0:T(8,128)(2,1)}, bf16[4,32,128]{2,1,0:T(8,128)(2,1)S(1)}, u32[]{:S(2)}, u32[]{:S(2)}) collective-permute-start(bf16[4,32,128]{2,1,0:T(8,128)(2,1)} %get-tuple-element.67), channel_id=1, source_target_pairs={{0,4},{1,5},{2,6},{3,7},{4,0},{5,1},{6,2},{7,3},{8,12},{9,13},{10,... | collective-permute-start | bytes 98312 | tf_op jit(solution)/shard_map/ppermute | solution.py:375
  89.3 8.2 %collective-permute-start.39 = (bf16[4,32,128]{2,1,0:T(8,128)(2,1)}, bf16[4,32,128]{2,1,0:T(8,128)(2,1)S(1)}, u32[]{:S(2)}, u32[]{:S(2)}) collective-permute-start(bf16[4,32,128]{2,1,0:T(8,128)(2,1)} %get-tuple-element.72.refs_0_.refs_4_), channel_id=1, source_target_pairs={{0,7},{1,0},{2,1},{3,2},{4,3},{5,4},{6,5},{7,6},{8,15},{9,8},{10,9... | collective-permute-start | bytes 98312 | tf_op jit(solution)/shard_map/ppermute | solution.py:375
  97.6 7.0 %collective-permute-start.34 = (bf16[4,32,128]{2,1,0:T(8,128)(2,1)}, bf16[4,32,128]{2,1,0:T(8,128)(2,1)S(1)}, u32[]{:S(2)}, u32[]{:S(2)}) collective-permute-start(bf16[4,32,128]{2,1,0:T(8,128)(2,1)} %get-tuple-element.72.refs_0_.refs_4_), channel_id=1, source_target_pairs={{0,2},{1,3},{2,4},{3,5},{4,6},{5,7},{6,0},{7,1},{8,10},{9,11},{10,... | collective-permute-start | bytes 98312 | tf_op jit(solution)/shard_map/ppermute | solution.py:375
  100.4 6.8 %collective-permute-start.33 = (bf16[4,32,128]{2,1,0:T(8,128)(2,1)}, bf16[4,32,128]{2,1,0:T(8,128)(2,1)S(1)}, u32[]{:S(2)}, u32[]{:S(2)}) collective-permute-start(bf16[4,32,128]{2,1,0:T(8,128)(2,1)} %get-tuple-element.72.refs_0_.refs_4_), channel_id=1, source_target_pairs={{0,1},{1,2},{2,3},{3,4},{4,5},{5,6},{6,7},{7,0},{8,9},{9,10},{10,1... | collective-permute-start | bytes 98312 | tf_op jit(solution)/shard_map/ppermute | solution.py:375
  100.4 6.8 %collective-permute-start.32 = (bf16[4,32,128]{2,1,0:T(8,128)(2,1)}, bf16[4,32,128]{2,1,0:T(8,128)(2,1)S(1)}, u32[]{:S(2)}, u32[]{:S(2)}) collective-permute-start(bf16[4,32,128]{2,1,0:T(8,128)(2,1)} %get-tuple-element.72.refs_0_.refs_4_), channel_id=1, source_target_pairs={{0,24},{8,0},{16,8},{24,16},{1,25},{9,1},{17,9},{25,17},{2,26},{10... | collective-permute-start | bytes 98312 | tf_op jit(solution)/shard_map/ppermute | solution.py:375
  118.4 7.0 %collective-permute-start.52 = (f32[32,128]{1,0:T(8,128)}, f32[32,128]{1,0:T(8,128)S(1)}, u32[]{:S(2)}, u32[]{:S(2)}) collective-permute-start(f32[32,128]{1,0:T(8,128)} %get-tuple-element.86.refs_0_), channel_id=1, source_target_pairs={{0,24},{8,0},{16,8},{24,16},{1,25},{9,1},{17,9},{25,17},{2,26},{10... | collective-permute-start | bytes 49160 | tf_op jit(solution)/shard_map/ppermute | solution.py:375
  130.3 7.9 %collective-permute-start.57 = (f32[32,128]{1,0:T(8,128)}, f32[32,128]{1,0:T(8,128)S(1)}, u32[]{:S(2)}, u32[]{:S(2)}) collective-permute-start(f32[32,128]{1,0:T(8,128)} %gram_sum.1.refs_12_), channel_id=1, source_target_pairs={{0,5},{1,6},{2,7},{3,0},{4,1},{5,2},{6,3},{7,4},{8,13},{9,14},{10,... | collective-permute-start | bytes 49160 | tf_op jit(solution)/shard_map/ppermute | solution.py:375
  130.3 7.8 %collective-permute-start.56 = (f32[32,128]{1,0:T(8,128)}, f32[32,128]{1,0:T(8,128)S(1)}, u32[]{:S(2)}, u32[]{:S(2)}) collective-permute-start(f32[32,128]{1,0:T(8,128)} %gram_sum.1.refs_12_), channel_id=1, source_target_pairs={{0,4},{1,5},{2,6},{3,7},{4,0},{5,1},{6,2},{7,3},{8,12},{9,13},{10,... | collective-permute-start | bytes 49160 | tf_op jit(solution)/shard_map/ppermute | solution.py:375
  136.8 6.6 %collective-permute-start.53 = (f32[32,128]{1,0:T(8,128)}, f32[32,128]{1,0:T(8,128)S(1)}, u32[]{:S(2)}, u32[]{:S(2)}) collective-permute-start(f32[32,128]{1,0:T(8,128)} %gram_sum.1.refs_12_), channel_id=1, source_target_pairs={{0,1},{1,2},{2,3},{3,4},{4,5},{5,6},{6,7},{7,0},{8,9},{9,10},{10,1... | collective-permute-start | bytes 49160 | tf_op jit(solution)/shard_map/ppermute | solution.py:375
  138.2 6.9 %collective-permute-start.41 = (bf16[4,32,128]{2,1,0:T(8,128)(2,1)}, bf16[4,32,128]{2,1,0:T(8,128)(2,1)S(1)}, u32[]{:S(2)}, u32[]{:S(2)}) collective-permute-start(bf16[4,32,128]{2,1,0:T(8,128)(2,1)} %get-tuple-element.76), channel_id=1, source_target_pairs={{0,16},{8,24},{16,0},{24,8},{1,17},{9,25},{17,1},{25,9},{2,18},{10... | collective-permute-start | bytes 98312 | tf_op jit(solution)/shard_map/ppermute | solution.py:375
  140.4 7.4 %collective-permute-start.42 = (bf16[4,32,128]{2,1,0:T(8,128)(2,1)}, bf16[4,32,128]{2,1,0:T(8,128)(2,1)S(1)}, u32[]{:S(2)}, u32[]{:S(2)}) collective-permute-start(bf16[4,32,128]{2,1,0:T(8,128)(2,1)} %get-tuple-element.77), channel_id=1, source_target_pairs={{0,24},{8,0},{16,8},{24,16},{1,25},{9,1},{17,9},{25,17},{2,26},{10... | collective-permute-start | bytes 98312 | tf_op jit(solution)/shard_map/ppermute | solution.py:375
  140.6 8.3 %collective-permute-start.43 = (bf16[4,32,128]{2,1,0:T(8,128)(2,1)}, bf16[4,32,128]{2,1,0:T(8,128)(2,1)S(1)}, u32[]{:S(2)}, u32[]{:S(2)}) collective-permute-start(bf16[4,32,128]{2,1,0:T(8,128)(2,1)} %get-tuple-element.79), channel_id=1, source_target_pairs={{0,1},{1,2},{2,3},{3,4},{4,5},{5,6},{6,7},{7,0},{8,9},{9,10},{10,1... | collective-permute-start | bytes 98312 | tf_op jit(solution)/shard_map/ppermute | solution.py:375
  143.4 7.7 %collective-permute-start.44 = (bf16[4,32,128]{2,1,0:T(8,128)(2,1)}, bf16[4,32,128]{2,1,0:T(8,128)(2,1)S(1)}, u32[]{:S(2)}, u32[]{:S(2)}) collective-permute-start(bf16[4,32,128]{2,1,0:T(8,128)(2,1)} %get-tuple-element.80), channel_id=1, source_target_pairs={{0,2},{1,3},{2,4},{3,5},{4,6},{5,7},{6,0},{7,1},{8,10},{9,11},{10,... | collective-permute-start | bytes 98312 | tf_op jit(solution)/shard_map/ppermute | solution.py:375
  143.4 9.7 %collective-permute-start.45 = (bf16[4,32,128]{2,1,0:T(8,128)(2,1)}, bf16[4,32,128]{2,1,0:T(8,128)(2,1)S(1)}, u32[]{:S(2)}, u32[]{:S(2)}) collective-permute-start(bf16[4,32,128]{2,1,0:T(8,128)(2,1)} %get-tuple-element.81), channel_id=1, source_target_pairs={{0,3},{1,4},{2,5},{3,6},{4,7},{5,0},{6,1},{7,2},{8,11},{9,12},{10,... | collective-permute-start | bytes 98312 | tf_op jit(solution)/shard_map/ppermute | solution.py:375
  145.0 8.1 %collective-permute-start.46 = (bf16[4,32,128]{2,1,0:T(8,128)(2,1)}, bf16[4,32,128]{2,1,0:T(8,128)(2,1)S(1)}, u32[]{:S(2)}, u32[]{:S(2)}) collective-permute-start(bf16[4,32,128]{2,1,0:T(8,128)(2,1)} %get-tuple-element.82), channel_id=1, source_target_pairs={{0,4},{1,5},{2,6},{3,7},{4,0},{5,1},{6,2},{7,3},{8,12},{9,13},{10,... | collective-permute-start | bytes 98312 | tf_op jit(solution)/shard_map/ppermute | solution.py:375
  (88 other events, 486.8 us)
